TPU v7x, 32 devices: a whole 2x2x4 slice. The times are simulated.
32 devices in a mesh: dp: 4 (over z), gx: 2 (over x), gy: 4 (over y, core).
Axes of the slice: x: 2, y: 2, z: 4, core: 2. Of those that a mesh axis runs over, the one named last changes fastest.
Arguments:
- volume: bfloat16 [4, 8, 64, 8, 128], P('dp', 'gx', 'gy'), may hold values from -6 to 6
- cotangent: bfloat16 [4, 8, 64, 8, 128], P('dp', 'gx', 'gy'), may hold values from -1 to 1
- master: float32 [6912, 128], P('dp'), may hold values from -0.109375 to 0.109375
- moment_one: float32 [6912, 128], P('dp'), may hold values from -6 to 6
- moment_two: float32 [6912, 128], P('dp'), may hold values from 0.25 to 4
Outputs:
- activation: bfloat16 [4, 8, 64, 8, 128], P('dp', 'gx', 'gy')
- new_master: float32 [6912, 128], P('dp')
- new_moment_one: float32 [6912, 128], P('dp')
- new_moment_two: float32 [6912, 128], P('dp')
All inputs are finite; a program needn't handle non-finite values.
Results may differ from a plain program's by a relative error of at most 0.006.
The roundings to bfloat16 on the way count: a program that leaves them out, or rounds other values in their place, can miss the bound.
Values may be sent and summed in bfloat16 or wider, within the bound.
A program may use at most 64 MiB of HBM per device.

v0:
```python
import jax
import jax.numpy as jnp
from jax import lax
from jax.sharding import PartitionSpec as P

inv_root_two = 0.7071067811865476
inv_root_tau = 0.3989422804014327
beta_one = 0.9
beta_two = 0.999
learn_rate = 0.01
epsilon = 1e-08


def extended(cells, sides, width):
    for axis, dim in sides:
        count = lax.axis_size(axis)
        ends = count - 1
        head = lax.slice_in_dim(cells, 0, width, axis=dim)
        tail = lax.slice_in_dim(cells, cells.shape[dim] - width, cells.shape[dim], axis=dim)
        cells = jnp.concatenate(
            [
                lax.ppermute(tail, axis, [(i, (i + 1) % count) for i in range(ends)]),
                cells,
                lax.ppermute(head, axis, [((i + 1) % count, i) for i in range(ends)]),
            ],
            axis=dim,
        )
    return cells


def gelu_value(field):
    return 0.5 * field * (1.0 + lax.erf(field * inv_root_two))


def gelu_slope(field):
    normal_cdf = 0.5 * (1.0 + lax.erf(field * inv_root_two))
    return normal_cdf + field * jnp.exp(-0.5 * field * field) * inv_root_tau


def depth_pad(field):
    return jnp.pad(field, ((0, 0), (0, 0), (1, 1), (0, 0)))


def convolve(padded, kernel, span_x, span_y, span_z):
    total = jnp.zeros((span_x * span_y * span_z, kernel.shape[2]), jnp.float32)
    for offset_x in range(3):
        for offset_y in range(3):
            for offset_z in range(3):
                window = padded[
                    offset_x : offset_x + span_x,
                    offset_y : offset_y + span_y,
                    offset_z : offset_z + span_z,
                ]
                total = total + jnp.dot(
                    window.reshape(-1, padded.shape[3]),
                    kernel[9 * offset_x + 3 * offset_y + offset_z],
                    preferred_element_type=jnp.float32,
                )
    return total


def weight_grad(padded, delta, span_x, span_y, span_z):
    pieces = []
    for offset_x in range(3):
        for offset_y in range(3):
            for offset_z in range(3):
                window = padded[
                    offset_x : offset_x + span_x,
                    offset_y : offset_y + span_y,
                    offset_z : offset_z + span_z,
                ]
                flat_window = window.reshape(-1, padded.shape[3])
                pieces.append(
                    lax.dot_general(
                        flat_window,
                        delta,
                        (((0,), (0,)), ((), ())),
                        preferred_element_type=jnp.float32,
                    )
                )
    return jnp.concatenate(pieces, axis=0)


def adam_update(master, moment_one, moment_two, gradient):
    new_one = beta_one * moment_one + (1.0 - beta_one) * gradient
    new_two = beta_two * moment_two + (1.0 - beta_two) * gradient * gradient
    update = new_one / (1.0 - beta_one**10) / (jnp.sqrt(new_two / (1.0 - beta_two**10)) + epsilon)
    return (master - learn_rate * update, new_one, new_two)


def per_device(volume, cotangent, master, moment_one, moment_two):
    field = volume[0]
    span_x, span_y, span_z, width = field.shape
    local_weights = master.astype(jnp.bfloat16)
    full_weights = lax.all_gather(local_weights, "dp", axis=0, tiled=True)
    kernels = full_weights.reshape(2, 27, width, width)
    flipped = kernels[1][::-1].transpose(0, 2, 1)
    padded_in = depth_pad(extended(field, (("gx", 0), ("gy", 1)), 1))
    first = convolve(padded_in, kernels[0], span_x, span_y, span_z)
    hidden = gelu_value(first).astype(jnp.bfloat16).reshape(span_x, span_y, span_z, width)
    padded_hidden = depth_pad(extended(hidden, (("gx", 0), ("gy", 1)), 1))
    second = convolve(padded_hidden, kernels[1], span_x, span_y, span_z)
    activation = gelu_value(second).astype(jnp.bfloat16).reshape(1, span_x, span_y, span_z, width)
    upstream = cotangent[0].reshape(span_x * span_y * span_z, width)
    delta_two = (upstream.astype(jnp.float32) * gelu_slope(second)).astype(jnp.bfloat16)
    grad_two = weight_grad(padded_hidden, delta_two, span_x, span_y, span_z)
    padded_delta = depth_pad(
        extended(delta_two.reshape(span_x, span_y, span_z, width), (("gx", 0), ("gy", 1)), 1)
    )
    back = convolve(padded_delta, flipped, span_x, span_y, span_z)
    delta_one = (back * gelu_slope(first)).astype(jnp.bfloat16)
    grad_one = weight_grad(padded_in, delta_one, span_x, span_y, span_z)
    gradient = jnp.concatenate([grad_one, grad_two], axis=0)
    summed = lax.psum(gradient, ("gx", "gy"))
    own_rows = lax.psum_scatter(
        summed.astype(jnp.bfloat16), "dp", scatter_dimension=0, tiled=True
    ).astype(jnp.float32)
    new_master, new_one, new_two = adam_update(master, moment_one, moment_two, own_rows)
    return (activation, new_master, new_one, new_two)


def solution(mesh):
    return jax.shard_map(
        per_device,
        mesh=mesh,
        in_specs=(
            P("dp", "gx", "gy", None, None),
            P("dp", "gx", "gy", None, None),
            P("dp", None),
            P("dp", None),
            P("dp", None),
        ),
        out_specs=(P("dp", "gx", "gy", None, None), P("dp", None), P("dp", None), P("dp", None)),
        check_vma=False,
    )
```

profile of v0, /device:TPU:1, one launch (start us, length us, event | category | flops | bytes accessed | tf_op | source)
XLA Modules:
  0.0 242.2 jit_solution(11026064678437312143)
XLA Ops:
  7.2 2.0 convert_element_type.31
  10.0 3.9 %collective-permute-start = (bf16[1,16,8,128]{3,2,1,0:T(8,128)(2,1)S(1)}, bf16[1,16,8,128]{3,2,1,0:T(8,128)(2,1)S(1)}, u32[]{:S(2)}, u32[]{:S(2)}) collective-permute-start(bf16[1,16,8,128]{3,2,1,0:T(8,128)(2,1)S(1)} %get-tuple-element.103), channel_id=1, source_target_pairs={{0,4},{1,5},{2,6},{3,7},{8,12},{9,13},{10,14},{11,15},{16,20},{17,... | collective-permute-start | bytes 98312 | tf_op jit(solution)/shard_map/ppermute | solution.py:22
  14.0 1.3 collective-permute-start.1
  15.3 3.3 %collective-permute-done.1 = bf16[1,16,8,128]{3,2,1,0:T(8,128)(2,1)S(1)} collective-permute-done((bf16[1,16,8,128]{3,2,1,0:T(8,128)(2,1)S(1)}, bf16[1,16,8,128]{3,2,1,0:T(8,128)(2,1)S(1)}, u32[]{:S(2)}, u32[]{:S(2)}) %collective-permute-start.1) | collective-permute-done | bytes 32800 | tf_op jit(solution)/shard_map/ppermute | solution.py:24
  19.4 5.1 %collective-permute-start.2 = (bf16[6,1,8,128]{3,2,1,0:T(8,128)(2,1)S(1)}, bf16[6,1,8,128]{3,2,1,0:T(8,128)(2,1)S(1)}, u32[]{:S(2)}, u32[]{:S(2)}) collective-permute-start(bf16[6,1,8,128]{3,2,1,0:T(8,128)(2,1)S(1)} %get-tuple-element.91), channel_id=1, source_target_pairs={{0,1},{1,2},{2,3},{4,5},{5,6},{6,7},{8,9},{9,10},{10,11},{12,13},{... | collective-permute-start | bytes 36872 | tf_op jit(solution)/shard_map/ppermute | solution.py:22
  24.5 1.9 collective-permute-start.3
  27.5 2.5 %collective-permute-done.3 = bf16[6,1,8,128]{3,2,1,0:T(8,128)(2,1)S(1)} collective-permute-done((bf16[6,1,8,128]{3,2,1,0:T(8,128)(2,1)S(1)}, bf16[6,1,8,128]{3,2,1,0:T(8,128)(2,1)S(1)}, u32[]{:S(2)}, u32[]{:S(2)}) %collective-permute-start.3) | collective-permute-done | bytes 12320 | tf_op jit(solution)/shard_map/ppermute | solution.py:24
  31.0 1.2 fusion.21
  32.9 19.7 %all-gather.2.cloned.1.call-done = bf16[6912,128]{1,0:T(8,128)(2,1)} async-done(((bf16[1728,128]{1,0:T(8,128)(2,1)}), bf16[6912,128]{1,0:T(8,128)(2,1)}) %all-gather.2.cloned.1.call-update) | async-done | bytes 1769488 | tf_op jit(solution)/shard_map/all_gather | solution.py:95
  63.2 3.1 %collective-permute-start.4 = (bf16[1,16,8,128]{3,2,1,0:T(8,128)(2,1)S(1)}, bf16[1,16,8,128]{3,2,1,0:T(8,128)(2,1)S(1)}, u32[]{:S(2)}, u32[]{:S(2)}) collective-permute-start(bf16[1,16,8,128]{3,2,1,0:T(8,128)(2,1)S(1)} %get-tuple-element.99), channel_id=1, source_target_pairs={{0,4},{1,5},{2,6},{3,7},{8,12},{9,13},{10,14},{11,15},{16,20},{17,... | collective-permute-start | bytes 98312 | tf_op jit(solution)/shard_map/ppermute | solution.py:22
  66.3 1.3 collective-permute-start.5
  67.6 3.3 %collective-permute-done.5 = bf16[1,16,8,128]{3,2,1,0:T(8,128)(2,1)S(1)} collective-permute-done((bf16[1,16,8,128]{3,2,1,0:T(8,128)(2,1)S(1)}, bf16[1,16,8,128]{3,2,1,0:T(8,128)(2,1)S(1)}, u32[]{:S(2)}, u32[]{:S(2)}) %collective-permute-start.5) | collective-permute-done | bytes 32800 | tf_op jit(solution)/shard_map/ppermute | solution.py:24
  70.9 5.1 %collective-permute-start.6 = (bf16[6,1,8,128]{3,2,1,0:T(8,128)(2,1)S(1)}, bf16[6,1,8,128]{3,2,1,0:T(8,128)(2,1)S(1)}, u32[]{:S(2)}, u32[]{:S(2)}) collective-permute-start(bf16[6,1,8,128]{3,2,1,0:T(8,128)(2,1)S(1)} %get-tuple-element.87), channel_id=1, source_target_pairs={{0,1},{1,2},{2,3},{4,5},{5,6},{6,7},{8,9},{9,10},{10,11},{12,13},{... | collective-permute-start | bytes 36872 | tf_op jit(solution)/shard_map/ppermute | solution.py:22
  76.1 1.9 collective-permute-start.7
  78.0 3.0 %collective-permute-done.7 = bf16[6,1,8,128]{3,2,1,0:T(8,128)(2,1)S(1)} collective-permute-done((bf16[6,1,8,128]{3,2,1,0:T(8,128)(2,1)S(1)}, bf16[6,1,8,128]{3,2,1,0:T(8,128)(2,1)S(1)}, u32[]{:S(2)}, u32[]{:S(2)}) %collective-permute-start.7) | collective-permute-done | bytes 12320 | tf_op jit(solution)/shard_map/ppermute | solution.py:24
  87.5 1.3 collective-permute-start.8
  88.9 1.3 collective-permute-start.9
  90.2 3.3 %collective-permute-done.9 = bf16[1,16,8,128]{3,2,1,0:T(8,128)(2,1)S(1)} collective-permute-done((bf16[1,16,8,128]{3,2,1,0:T(8,128)(2,1)S(1)}, bf16[1,16,8,128]{3,2,1,0:T(8,128)(2,1)S(1)}, u32[]{:S(2)}, u32[]{:S(2)}) %collective-permute-start.9) | collective-permute-done | bytes 32800 | tf_op jit(solution)/shard_map/ppermute | solution.py:24
  93.5 3.4 %collective-permute-start.10 = (bf16[6,1,8,128]{3,2,1,0:T(8,128)(2,1)S(1)}, bf16[6,1,8,128]{3,2,1,0:T(8,128)(2,1)S(1)}, u32[]{:S(2)}, u32[]{:S(2)}) collective-permute-start(bf16[6,1,8,128]{3,2,1,0:T(8,128)(2,1)S(1)} %get-tuple-element.83), channel_id=1, source_target_pairs={{0,1},{1,2},{2,3},{4,5},{5,6},{6,7},{8,9},{9,10},{10,11},{12,13},{... | collective-permute-start | bytes 36872 | tf_op jit(solution)/shard_map/ppermute | solution.py:22
  96.9 2.1 collective-permute-start.11
  99.1 2.9 %collective-permute-done.11 = bf16[6,1,8,128]{3,2,1,0:T(8,128)(2,1)S(1)} collective-permute-done((bf16[6,1,8,128]{3,2,1,0:T(8,128)(2,1)S(1)}, bf16[6,1,8,128]{3,2,1,0:T(8,128)(2,1)S(1)}, u32[]{:S(2)}, u32[]{:S(2)}) %collective-permute-start.11) | collective-permute-done | bytes 12320 | tf_op jit(solution)/shard_map/ppermute | solution.py:24
  121.2 74.1 %all-reduce.4 = bf16[6912,128]{1,0:T(8,128)(2,1)} all-reduce(f32[6912,128]{1,0:T(8,128)S(1)} %convolution_dynamic-update-slice_fusion), channel_id=1, replica_groups=mesh['dp'=4,'gx'=2,'gy'=4] {'gx','gy'}, use_global_device_ids=true, to_apply=%region_0.1 | all-reduce | flops 884736 | bytes 5308416 | tf_op jit(solution)/shard_map/psum | solution.py:114
  195.3 36.4 %reduce-scatter.2.cloned.1.call-done = bf16[1728,128]{1,0:T(8,128)(2,1)} async-done(((bf16[6912,128]{1,0:T(8,128)(2,1)}), bf16[1728,128]{1,0:T(8,128)(2,1)}) %reduce-scatter.2.cloned.1.call-update) | async-done | bytes 442384 | tf_op jit(solution)/shard_map/reduce_scatter | solution.py:115
  231.7 3.7 %multiply_subtract_fusion = (f32[1728,128]{1,0:T(8,128)}, f32[1728,128]{1,0:T(8,128)}, f32[1728,128]{1,0:T(8,128)}) fusion(f32[1728,128]{1,0:T(8,128)} %param.7, bf16[1728,128]{1,0:T(8,128)(2,1)} %reduce-scatter.2.cloned.1.call-done, f32[1728,128]{1,0:T(8,128)} %param.8, f32[1728,128]{1,0:T(8,128)} %param.9), kind=kLoop, calls=%fused_computation.141 | loop fusion | flops 3096576 | bytes 5750784 | tf_op jit(solution)/shard_map/sub | solution.py:88
  (280 shorter events, 39.0 us)
Async XLA Ops:
  7.2 45.4 %all-gather.2.cloned.1.call-start = ((), (), s32[]{:S(2)}) async-start(), calls=%async_computation.1 | async-start | bytes 2211840 | tf_op jit(solution)/shard_map/all_gather | solution.py:95
  9.2 222.5 %reduce-scatter.2.cloned.1.call-start = ((), (), s32[]{:S(2)}) async-start(), calls=%async_computation.2 | async-start | bytes 2211840 | tf_op jit(solution)/shard_map/reduce_scatter | solution.py:115
  10.0 5.2 %collective-permute-start = (bf16[1,16,8,128]{3,2,1,0:T(8,128)(2,1)S(1)}, bf16[1,16,8,128]{3,2,1,0:T(8,128)(2,1)S(1)}, u32[]{:S(2)}, u32[]{:S(2)}) collective-permute-start(bf16[1,16,8,128]{3,2,1,0:T(8,128)(2,1)S(1)} %get-tuple-element.103), channel_id=1, source_target_pairs={{0,4},{1,5},{2,6},{3,7},{8,12},{9,13},{10,14},{11,15},{16,20},{17,... | collective-permute-start | bytes 98312 | tf_op jit(solution)/shard_map/ppermute | solution.py:22
  14.0 4.7 %collective-permute-start.1 = (bf16[1,16,8,128]{3,2,1,0:T(8,128)(2,1)S(1)}, bf16[1,16,8,128]{3,2,1,0:T(8,128)(2,1)S(1)}, u32[]{:S(2)}, u32[]{:S(2)}) collective-permute-start(bf16[1,16,8,128]{3,2,1,0:T(8,128)(2,1)S(1)} %get-tuple-element.104), channel_id=1, source_target_pairs={{4,0},{5,1},{6,2},{7,3},{12,8},{13,9},{14,10},{15,11},{20,16},{21,... | collective-permute-start | bytes 98312 | tf_op jit(solution)/shard_map/ppermute | solution.py:24
  19.4 8.1 %collective-permute-start.2 = (bf16[6,1,8,128]{3,2,1,0:T(8,128)(2,1)S(1)}, bf16[6,1,8,128]{3,2,1,0:T(8,128)(2,1)S(1)}, u32[]{:S(2)}, u32[]{:S(2)}) collective-permute-start(bf16[6,1,8,128]{3,2,1,0:T(8,128)(2,1)S(1)} %get-tuple-element.91), channel_id=1, source_target_pairs={{0,1},{1,2},{2,3},{4,5},{5,6},{6,7},{8,9},{9,10},{10,11},{12,13},{... | collective-permute-start | bytes 36872 | tf_op jit(solution)/shard_map/ppermute | solution.py:22
  24.5 5.4 %collective-permute-start.3 = (bf16[6,1,8,128]{3,2,1,0:T(8,128)(2,1)S(1)}, bf16[6,1,8,128]{3,2,1,0:T(8,128)(2,1)S(1)}, u32[]{:S(2)}, u32[]{:S(2)}) collective-permute-start(bf16[6,1,8,128]{3,2,1,0:T(8,128)(2,1)S(1)} %get-tuple-element.92), channel_id=1, source_target_pairs={{1,0},{2,1},{3,2},{5,4},{6,5},{7,6},{9,8},{10,9},{11,10},{13,12},{... | collective-permute-start | bytes 36872 | tf_op jit(solution)/shard_map/ppermute | solution.py:24
  27.4 30.9 %copy-start.52 = (bf16[4,16,8,128]{3,2,1,0:T(8,128)(2,1)}, bf16[4,16,8,128]{3,2,1,0:T(8,128)(2,1)S(1)}, u32[]{:S(2)}) copy-start(bf16[4,16,8,128]{3,2,1,0:T(8,128)(2,1)S(1)} %get-tuple-element.102) | copy-start | bytes 393220
  27.4 34.9 %copy-start.50 = (bf16[4,16,8,128]{3,2,1,0:T(8,128)(2,1)}, bf16[4,16,8,128]{3,2,1,0:T(8,128)(2,1)S(1)}, u32[]{:S(2)}) copy-start(bf16[4,16,8,128]{3,2,1,0:T(8,128)(2,1)S(1)} %get-tuple-element.101) | copy-start | bytes 393220
  32.3 28.9 %copy-start.16 = (bf16[4,16,8,128]{3,2,1,0:T(8,128)(2,1)}, bf16[4,16,8,128]{3,2,1,0:T(8,128)(2,1)S(1)}, u32[]{:S(2)}) copy-start(bf16[4,16,8,128]{3,2,1,0:T(8,128)(2,1)S(1)} %get-tuple-element.76) | copy-start | bytes 393220
  32.3 29.5 %copy-start.12 = (bf16[4,16,8,128]{3,2,1,0:T(8,128)(2,1)}, bf16[4,16,8,128]{3,2,1,0:T(8,128)(2,1)S(1)}, u32[]{:S(2)}) copy-start(bf16[4,16,8,128]{3,2,1,0:T(8,128)(2,1)S(1)} %get-tuple-element.109) | copy-start | bytes 393220
  32.4 30.4 %copy-start.10 = (bf16[4,16,8,128]{3,2,1,0:T(8,128)(2,1)}, bf16[4,16,8,128]{3,2,1,0:T(8,128)(2,1)S(1)}, u32[]{:S(2)}) copy-start(bf16[4,16,8,128]{3,2,1,0:T(8,128)(2,1)S(1)} %get-tuple-element.75) | copy-start | bytes 393220
  32.9 28.7 %copy-start.22 = (bf16[4,16,8,128]{3,2,1,0:T(8,128)(2,1)}, bf16[4,16,8,128]{3,2,1,0:T(8,128)(2,1)S(1)}, u32[]{:S(2)}) copy-start(bf16[4,16,8,128]{3,2,1,0:T(8,128)(2,1)S(1)} %get-tuple-element.48) | copy-start | bytes 393220
  32.9 29.1 %copy-start.20 = (bf16[4,16,8,128]{3,2,1,0:T(8,128)(2,1)}, bf16[4,16,8,128]{3,2,1,0:T(8,128)(2,1)S(1)}, u32[]{:S(2)}) copy-start(bf16[4,16,8,128]{3,2,1,0:T(8,128)(2,1)S(1)} %get-tuple-element.47) | copy-start | bytes 393220
  32.9 29.3 %copy-start.18 = (bf16[4,16,8,128]{3,2,1,0:T(8,128)(2,1)}, bf16[4,16,8,128]{3,2,1,0:T(8,128)(2,1)S(1)}, u32[]{:S(2)}) copy-start(bf16[4,16,8,128]{3,2,1,0:T(8,128)(2,1)S(1)} %get-tuple-element.46) | copy-start | bytes 393220
  32.9 29.7 %copy-start.14 = (bf16[4,16,8,128]{3,2,1,0:T(8,128)(2,1)}, bf16[4,16,8,128]{3,2,1,0:T(8,128)(2,1)S(1)}, u32[]{:S(2)}) copy-start(bf16[4,16,8,128]{3,2,1,0:T(8,128)(2,1)S(1)} %get-tuple-element.44) | copy-start | bytes 393220
  32.9 30.0 %copy-start.2 = (bf16[4,16,8,128]{3,2,1,0:T(8,128)(2,1)}, bf16[4,16,8,128]{3,2,1,0:T(8,128)(2,1)S(1)}, u32[]{:S(2)}) copy-start(bf16[4,16,8,128]{3,2,1,0:T(8,128)(2,1)S(1)} %get-tuple-element.43) | copy-start | bytes 393220
  63.2 4.4 %collective-permute-start.4 = (bf16[1,16,8,128]{3,2,1,0:T(8,128)(2,1)S(1)}, bf16[1,16,8,128]{3,2,1,0:T(8,128)(2,1)S(1)}, u32[]{:S(2)}, u32[]{:S(2)}) collective-permute-start(bf16[1,16,8,128]{3,2,1,0:T(8,128)(2,1)S(1)} %get-tuple-element.99), channel_id=1, source_target_pairs={{0,4},{1,5},{2,6},{3,7},{8,12},{9,13},{10,14},{11,15},{16,20},{17,... | collective-permute-start | bytes 98312 | tf_op jit(solution)/shard_map/ppermute | solution.py:22
  66.3 4.7 %collective-permute-start.5 = (bf16[1,16,8,128]{3,2,1,0:T(8,128)(2,1)S(1)}, bf16[1,16,8,128]{3,2,1,0:T(8,128)(2,1)S(1)}, u32[]{:S(2)}, u32[]{:S(2)}) collective-permute-start(bf16[1,16,8,128]{3,2,1,0:T(8,128)(2,1)S(1)} %get-tuple-element.100), channel_id=1, source_target_pairs={{4,0},{5,1},{6,2},{7,3},{12,8},{13,9},{14,10},{15,11},{20,16},{21,... | collective-permute-start | bytes 98312 | tf_op jit(solution)/shard_map/ppermute | solution.py:24
  70.9 7.1 %collective-permute-start.6 = (bf16[6,1,8,128]{3,2,1,0:T(8,128)(2,1)S(1)}, bf16[6,1,8,128]{3,2,1,0:T(8,128)(2,1)S(1)}, u32[]{:S(2)}, u32[]{:S(2)}) collective-permute-start(bf16[6,1,8,128]{3,2,1,0:T(8,128)(2,1)S(1)} %get-tuple-element.87), channel_id=1, source_target_pairs={{0,1},{1,2},{2,3},{4,5},{5,6},{6,7},{8,9},{9,10},{10,11},{12,13},{... | collective-permute-start | bytes 36872 | tf_op jit(solution)/shard_map/ppermute | solution.py:22
  76.1 5.0 %collective-permute-start.7 = (bf16[6,1,8,128]{3,2,1,0:T(8,128)(2,1)S(1)}, bf16[6,1,8,128]{3,2,1,0:T(8,128)(2,1)S(1)}, u32[]{:S(2)}, u32[]{:S(2)}) collective-permute-start(bf16[6,1,8,128]{3,2,1,0:T(8,128)(2,1)S(1)} %get-tuple-element.88), channel_id=1, source_target_pairs={{1,0},{2,1},{3,2},{5,4},{6,5},{7,6},{9,8},{10,9},{11,10},{13,12},{... | collective-permute-start | bytes 36872 | tf_op jit(solution)/shard_map/ppermute | solution.py:24
  87.5 2.7 %collective-permute-start.8 = (bf16[1,16,8,128]{3,2,1,0:T(8,128)(2,1)S(1)}, bf16[1,16,8,128]{3,2,1,0:T(8,128)(2,1)S(1)}, u32[]{:S(2)}, u32[]{:S(2)}) collective-permute-start(bf16[1,16,8,128]{3,2,1,0:T(8,128)(2,1)S(1)} %get-tuple-element.95), channel_id=1, source_target_pairs={{0,4},{1,5},{2,6},{3,7},{8,12},{9,13},{10,14},{11,15},{16,20},{17,... | collective-permute-start | bytes 98312 | tf_op jit(solution)/shard_map/ppermute | solution.py:22
  88.9 4.7 %collective-permute-start.9 = (bf16[1,16,8,128]{3,2,1,0:T(8,128)(2,1)S(1)}, bf16[1,16,8,128]{3,2,1,0:T(8,128)(2,1)S(1)}, u32[]{:S(2)}, u32[]{:S(2)}) collective-permute-start(bf16[1,16,8,128]{3,2,1,0:T(8,128)(2,1)S(1)} %get-tuple-element.96), channel_id=1, source_target_pairs={{4,0},{5,1},{6,2},{7,3},{12,8},{13,9},{14,10},{15,11},{20,16},{21,... | collective-permute-start | bytes 98312 | tf_op jit(solution)/shard_map/ppermute | solution.py:24
  93.5 5.5 %collective-permute-start.10 = (bf16[6,1,8,128]{3,2,1,0:T(8,128)(2,1)S(1)}, bf16[6,1,8,128]{3,2,1,0:T(8,128)(2,1)S(1)}, u32[]{:S(2)}, u32[]{:S(2)}) collective-permute-start(bf16[6,1,8,128]{3,2,1,0:T(8,128)(2,1)S(1)} %get-tuple-element.83), channel_id=1, source_target_pairs={{0,1},{1,2},{2,3},{4,5},{5,6},{6,7},{8,9},{9,10},{10,11},{12,13},{... | collective-permute-start | bytes 36872 | tf_op jit(solution)/shard_map/ppermute | solution.py:22
  96.9 5.0 %collective-permute-start.11 = (bf16[6,1,8,128]{3,2,1,0:T(8,128)(2,1)S(1)}, bf16[6,1,8,128]{3,2,1,0:T(8,128)(2,1)S(1)}, u32[]{:S(2)}, u32[]{:S(2)}) collective-permute-start(bf16[6,1,8,128]{3,2,1,0:T(8,128)(2,1)S(1)} %get-tuple-element.84), channel_id=1, source_target_pairs={{1,0},{2,1},{3,2},{5,4},{6,5},{7,6},{9,8},{10,9},{11,10},{13,12},{... | collective-permute-start | bytes 36872 | tf_op jit(solution)/shard_map/ppermute | solution.py:24
  (46 other events, 559.5 us)
Sparse Core Ops, SparseCore 0:
  10.1 42.3 all-gather.1
  195.4 36.2 reduce-scatter.1
where the time goes:
time: 244 us; the launch traced here: 242 us
  waiting for transfers between devices  74.4 us (30%)
  blocking collectives  74.1 us (30%)
  matrix products  32.8 us (13%)
  starting transfers between devices  31.8 us (13%)
  between operations  16.2 us (7%)
  other arithmetic  10.4 us (4%)
  local copies, waits for them, and re-layouts  2.59 us (1%)
    psum x1, blocking collectives, per_device(): summed = lax.psum(gradient, ('gx', 'gy'))  74.1 us
    reduce_scatter x1, waiting for transfers between devices, per_device(): lax.psum_scatter(summed.astype(jnp.bfloat16), 'dp', scatter_dimension=0,...  36.4 us
    ppermute x6, starting transfers between devices, extended(): lax.ppermute(tail, axis, [(i, (i + 1) % count) for i in range(ends)])  21.9 us
    dot_general x81, matrix products, convolve(): jnp.dot(window.reshape(-1, padded.shape[3]), kernel[9 * offset_x + 3 * of...  20.5 us
    all_gather x1, waiting for transfers between devices, per_device(): full_weights = lax.all_gather(local_weights, 'dp', axis=0, tiled=True)  19.7 us
    ppermute x6, waiting for transfers between devices, extended(): lax.ppermute(head, axis, [((i + 1) % count, i) for i in range(ends)])  18.3 us
    dot_general x54, matrix products, weight_grad(): lax.dot_general(flat_window, delta, (((0,), (0,)), ((), ())), preferred_e...  12.3 us
    ppermute x6, starting transfers between devices, extended(): lax.ppermute(head, axis, [((i + 1) % count, i) for i in range(ends)])  9.82 us
  transfers between devices with their start and end apart: 14, of which 8 were waited for; matrix products, arithmetic and copies ran while one was open for 2% of the time, Pallas kernels for 0%

commit v1 on v0

v1 whole, which is shorter than its diff:
```python
import functools

import jax
import jax.numpy as jnp
from jax import lax
from jax.experimental import pallas as pl
from jax.experimental.pallas import tpu as pltpu
from jax.sharding import PartitionSpec as P

inv_root_two = 0.7071067811865476
inv_root_tau = 0.3989422804014327
beta_one = 0.9
beta_two = 0.999
learn_rate = 0.01
epsilon = 1e-08
C = 128
HX, HY, CY = 3, 4, 2
MESH = pl.DeviceIdType.MESH
VMEM = pltpu.VMEM
f32, bf16 = jnp.float32, jnp.bfloat16


def gelu_value(field):
    return 0.5 * field * (1.0 + lax.erf(field * inv_root_two))


def gelu_slope(field):
    normal_cdf = 0.5 * (1.0 + lax.erf(field * inv_root_two))
    return normal_cdf + field * jnp.exp(-0.5 * field * field) * inv_root_tau


def place():
    d, x, y = lax.axis_index("dp"), lax.axis_index("gx"), lax.axis_index("gy")
    return d, x, y, lax.rem(x, 2), lax.rem(lax.div(y, 2), 2), lax.rem(y, 2)


def flip(index, bit, step):
    return index + step - 2 * step * bit


def gather_kernel(counts, vol, cot, master, vext, cext, w, hsend, hrecv, wsend, wrecv):
    D, GX, GY = counts
    d, x, y, bx, by, bc = place()
    sx, ry = vol.shape[0], vol.shape[1]
    H = master.shape[0]
    Q = H // 4
    here = {"x": (d, flip(x, bx, 1), y), "y": (d, x, flip(y, by, 2)), "c": (d, x, flip(y, bc, 1))}

    vext[...] = jnp.zeros_like(vext)
    cext[...] = jnp.zeros_like(cext)
    around = [(i, j) for i in (-1, 0, 1) for j in (-1, 0, 1) if (i, j) != (0, 0)]

    def exists(i, j):
        ok = None
        for value, step, count in ((x, i, GX), (y, j, GY)):
            if step:
                now = (value + step >= 0) & (value + step < count)
                ok = now if ok is None else ok & now
        return ok

    barrier = pltpu.get_barrier_semaphore()
    total = jnp.int32(3)
    for key in ("x", "y", "c"):
        pl.semaphore_signal(barrier, inc=1, device_id=here[key], device_id_type=MESH)
    for i, j in around:
        ok = exists(i, j)

        @pl.when(ok)
        def _(i=i, j=j):
            pl.semaphore_signal(barrier, inc=1, device_id=(d, x + i, y + j), device_id_type=MESH)

        total = total + jnp.where(ok, 1, 0)
    for step in (-1, 1):
        ok = (d + step >= 0) & (d + step < D)

        @pl.when(ok)
        def _(step=step):
            pl.semaphore_signal(barrier, inc=1, device_id=(d + step, x, y), device_id_type=MESH)

        total = total + jnp.where(ok, 1, 0)

    vext[pl.ds(HX, sx), pl.ds(8 * HY, ry)] = vol[...]
    cext[pl.ds(1, sx), pl.ds(8 * CY, ry)] = cot[...]
    w[pl.ds(pl.multiple_of(d * H, 16), H)] = master[...].astype(bf16)
    pl.semaphore_wait(barrier, total)

    def rows(s, q):
        return w.at[pl.ds(pl.multiple_of(s * H + q * Q, 16), Q)]

    def move(ref, k, s, target):
        return pltpu.make_async_remote_copy(
            src_ref=ref, dst_ref=ref, send_sem=wsend.at[k, s], recv_sem=wrecv.at[k, s],
            device_id=target, device_id_type=MESH,
        )

    def bit(s):
        even = lax.rem(s, 2) == 0
        return even, jnp.where(even, bx, by)

    def quarter(s):
        return 2 * bit(s)[1] + bc

    def other(s):
        return 2 * (1 - bit(s)[1]) + bc

    def up(s):
        return move(rows(s, quarter(s)), 0, s, (d + 1, x, y))

    def down(s):
        return move(rows(s, quarter(s)), 1, s, (d - 1, x, y))

    def partner(s, q):
        even = lax.rem(s, 2) == 0
        target = (d, jnp.where(even, here["x"][1], x), jnp.where(even, y, here["y"][2]))
        return move(rows(s, q), 2, s, target)

    def sibling(s, q, k):
        return move(rows(s, q), k, s, here["c"])

    @pl.when(d < D - 1)
    def _():
        up(d).start()

    @pl.when(d > 0)
    def _():
        down(d).start()

    def halo(n, i, j):
        def part(step, halo_x, size):
            if step < 0:
                return 0, halo_x + size, halo_x
            if step > 0:
                return size - halo_x, 0, halo_x
            return 0, halo_x, size

        copies = []
        for k, (src, dst, hx, hy) in enumerate(((vol, vext, HX, HY), (cot, cext, 1, CY))):
            xs, xd, xn = part(i, hx, sx)
            ys, yd, yn = part(j, 8 * hy, ry)
            copies.append(
                pltpu.make_async_remote_copy(
                    src_ref=src.at[pl.ds(xs, xn), pl.ds(ys, yn)],
                    dst_ref=dst.at[pl.ds(xd, xn), pl.ds(yd, yn)],
                    send_sem=hsend.at[k, n], recv_sem=hrecv.at[k, n],
                    device_id=(d, x + i, y + j), device_id_type=MESH,
                )
            )
        return copies

    for n, (i, j) in enumerate(around):
        @pl.when(exists(i, j))
        def _(n=n, i=i, j=j):
            for copy in halo(n, i, j):
                copy.start()

    def spread(s):
        partner(s, quarter(s)).start()
        sibling(s, quarter(s), 3).start()

    def pass_on(s):
        partner(s, other(s)).wait_recv()
        sibling(s, other(s), 4).start()

    for t in range(1, D):
        @pl.when(d - t >= 0)
        def _(t=t):
            s = d - t
            up(s).wait_recv()

            @pl.when(d < D - 1)
            def _():
                up(s).start()

            spread(s)

        @pl.when(d + t < D)
        def _(t=t):
            s = d + t
            down(s).wait_recv()

            @pl.when(d > 0)
            def _():
                down(s).start()

            spread(s)

        if t > 1:
            @pl.when(d - t + 1 >= 0)
            def _(t=t):
                pass_on(d - t + 1)

            @pl.when(d + t - 1 < D)
            def _(t=t):
                pass_on(d + t - 1)

    @pl.when(d - D + 1 >= 0)
    def _():
        pass_on(d - D + 1)

    @pl.when(d + D - 1 < D)
    def _():
        pass_on(d + D - 1)

    for t in range(1, D):
        for sign in (-1, 1):
            s = d + sign * t

            @pl.when((s >= 0) & (s < D))
            def _(s=s):
                theirs = 2 * bit(s)[1] + 1 - bc
                sibling(s, theirs, 3).wait_recv()
                sibling(s, 2 * (1 - bit(s)[1]) + 1 - bc, 4).wait_recv()
                partner(s, quarter(s)).wait_send()
                sibling(s, quarter(s), 3).wait_send()
                sibling(s, other(s), 4).wait_send()

    for s in range(D):
        @pl.when((s <= d) & (d < D - 1))
        def _(s=s):
            up(jnp.int32(s)).wait_send()

        @pl.when((s >= d) & (d > 0))
        def _(s=s):
            down(jnp.int32(s)).wait_send()

    for n, (i, j) in enumerate(around):
        @pl.when(exists(i, j))
        def _(n=n, i=i, j=j):
            for copy in halo(n, i, j):
                copy.wait_send()
            for copy in halo(7 - n, -i, -j):
                copy.wait_recv()


def shifted(field):
    rows = field.shape[0]
    z = lax.rem(lax.broadcasted_iota(jnp.int32, field.shape, 0), 8)
    before = jnp.where(z == 0, 0.0, pltpu.roll(field, 1, 0))
    after = jnp.where(z == 7, 0.0, pltpu.roll(field, rows - 1, 0))
    return before, field, after


def unfold(field, first, rows, out):
    views = shifted(field)
    for b in range(3):
        for c in range(3):
            k = 3 * b + c
            out[:, k * C : (k + 1) * C] = views[c][first + 8 * b : first + 8 * b + rows].astype(bf16)


def compute_kernel(counts, vext, cext, w, act, grad, x1, x2, x3, first, kt, d1, d2):
    D, GX, GY = counts
    sx = vext.shape[0] - 2 * HX
    ry = vext.shape[1] - 16 * HY
    gx, gy = lax.axis_index("gx"), lax.axis_index("gy")
    n1, n2 = ry + 32, ry + 16
    L = 9 * C

    d1[...] = jnp.zeros_like(d1)
    d2[...] = jnp.zeros_like(d2)

    @pl.loop(0, sx + 6)
    def _(s):
        unfold(vext[s].astype(f32), 8, n1, x1.at[s])

    for a in range(3):
        for k in range(9):
            base = (27 + 9 * (2 - a) + 8 - k) * C
            kt[a, :, k * C : (k + 1) * C] = w[base : base + C]

    def conv(source, kernel, at, size, contract):
        total = None
        for a in range(3):
            lhs = source[pl.ds(at + a, size)]
            lhs = lhs.reshape(size * lhs.shape[1], L)
            term = lax.dot_general(
                lhs, kernel(a), (((1,), (contract,)), ((), ())), preferred_element_type=f32
            )
            total = term if total is None else total + term
        return total

    half = (sx + 4) // 2
    row = lax.broadcasted_iota(jnp.int32, (n1, C), 0)
    y_at = lax.div(row, 8) - 2 + gy * (ry // 8)
    y_ok = jnp.where((y_at >= 0) & (y_at < GY * (ry // 8)), 1.0, 0.0)

    @pl.loop(0, 2)
    def _(p):
        pre = conv(x1, lambda a: w[a * L : (a + 1) * L], p * half, half, 0)
        for i in range(half):
            piece = pre[i * n1 : (i + 1) * n1]
            s = p * half + i
            first[s] = piece
            x_at = s - 2 + gx * sx
            x_ok = jnp.where((x_at >= 0) & (x_at < GX * sx), 1.0, 0.0)
            hidden = gelu_value(piece).astype(bf16).astype(f32) * (y_ok * x_ok)
            unfold(hidden, 0, n2, x2.at[s])

    half2 = (sx + 2) // 2

    @pl.loop(0, 2)
    def _(p):
        pre = conv(x2, lambda a: w[27 * C + a * L : 27 * C + (a + 1) * L], p * half2, half2, 0)
        for i in range(half2):
            piece = pre[i * n2 : (i + 1) * n2]
            s = p * half2 + i
            up = cext[s].astype(f32)[8 : 8 + n2]
            delta = (up * gelu_slope(piece)).astype(bf16).astype(f32)
            unfold(delta, 0, ry, x3.at[s])

            @pl.when((s >= 1) & (s <= sx))
            def _():
                act[s - 1] = gelu_value(piece)[8 : 8 + ry].astype(bf16)
                r2 = lax.broadcasted_iota(jnp.int32, (n2, C), 0)
                inner = jnp.where((r2 >= 8) & (r2 < 8 + ry), delta, 0.0).astype(bf16)
                for a in range(3):
                    d2[s - 1 + a, :, a * C : (a + 1) * C] = inner

    def weight_grad(source, start, delta, base):
        n = delta.shape[1]
        rhs = delta[...].reshape((sx + 2) * n, 3 * C)

        @pl.loop(0, 3)
        def _(m):
            lanes = pl.ds(pl.multiple_of(m * 3 * C, C), 3 * C)
            lhs = source[pl.ds(start, sx + 2), :, lanes].reshape((sx + 2) * n, 3 * C)
            out = lax.dot_general(lhs, rhs, (((0,), (0,)), ((), ())), preferred_element_type=f32)
            for a in range(3):
                at = pl.multiple_of(base + a * L + m * 3 * C, C)
                grad[pl.ds(at, 3 * C)] = out[:, a * C : (a + 1) * C].astype(bf16)

    weight_grad(x2, 1, d2, 27 * C)

    back = conv(x3, lambda a: kt[a], 0, sx, 1)
    for i in range(sx):
        piece = back[i * ry : (i + 1) * ry]
        slope = gelu_slope(first[i + 2][16 : 16 + ry])
        delta = (piece * slope).astype(bf16)
        for a in range(3):
            d1[i + a, 16 : 16 + ry, a * C : (a + 1) * C] = delta
    weight_grad(x1, 2, d1, 0)


def reduce_kernel(counts, g, out, r1, a1, r2, a2, r3, a3, r4, fin, s1, q1, s2, q2, s3, q3, s4, q4, s5, q5, s6, q6):
    D, GX, GY = counts
    d, x, y, bx, by, bc = place()
    H = out.shape[0]
    Q = H // 4
    cut = Q // 32 * 16
    px, py, pc = (d, flip(x, bx, 1), y), (d, x, flip(y, by, 2)), (d, x, flip(y, bc, 1))
    pxy = (d, flip(x, bx, 1), flip(y, by, 2))

    barrier = pltpu.get_barrier_semaphore()
    for target in (px, py, pc, pxy):
        pl.semaphore_signal(barrier, inc=1, device_id=target, device_id_type=MESH)
    for t in range(1, D):
        pl.semaphore_signal(barrier, inc=1, device_id=(lax.rem(d + t, D), x, y), device_id_type=MESH)
    pl.semaphore_wait(barrier, 4 + D - 1)

    def copy(src, dst, send, recv, target):
        return pltpu.make_async_remote_copy(
            src_ref=src, dst_ref=dst, send_sem=send, recv_sem=recv, device_id=target, device_id_type=MESH
        )

    def quarter(s, q):
        return pl.ds(pl.multiple_of(s * H + q * Q, 16), Q)

    def stage1(s, b):
        return copy(g.at[quarter(s, 2 * b + 1 - bc)], r1.at[s, b], s1.at[s, b], q1.at[s, b], pc)

    def bits(s):
        return (bx, by, px, py) if s % 2 == 0 else (by, bx, py, px)

    def stage2(s):
        b, _, target, _ = bits(s)
        return copy(a1.at[s, 1 - b], r2.at[s], s2.at[s], q2.at[s], target)

    def halves(bit, body):
        @pl.when(bit == 0)
        def _():
            body(0, cut, cut, Q - cut)

        @pl.when(bit == 1)
        def _():
            body(cut, Q - cut, 0, cut)

    def stage3(s, lo, n):
        target = bits(s)[3]
        return copy(a2.at[s, pl.ds(lo, n)], r3.at[s, pl.ds(lo, n)], s3.at[s], q3.at[s], target)

    for s in range(D):
        for b in range(2):
            stage1(s, b).start()
    for s in range(D):
        for b in range(2):
            stage1(s, b).wait_recv()
            a1[s, b] = (g[quarter(s, 2 * b + bc)].astype(f32) + r1[s, b].astype(f32)).astype(bf16)
        stage2(s).start()
    for s in range(D):
        stage2(s).wait_recv()
        b = bits(s)[0]
        a2[s] = (a1[s, b].astype(f32) + r2[s].astype(f32)).astype(bf16)

        def send(lo, n, olo, on, s=s):
            stage3(s, olo, on).start()

        halves(bits(s)[1], send)

    def stage4(s, t, lo, n):
        return copy(a3.at[s, pl.ds(lo, n)], r4.at[t - 1, pl.ds(lo, n)], s4.at[t - 1], q4.at[t - 1], (s, x, y))

    for s in range(D):
        def add(lo, n, olo, on, s=s):
            stage3(s, lo, n).wait_recv()
            at = pl.ds(lo, n)
            a3[s, at] = (a2[s, at].astype(f32) + r3[s, at].astype(f32)).astype(bf16)
            for t in range(1, D):
                @pl.when(lax.rem(d + t, D) == s)
                def _(t=t):
                    stage4(s, t, lo, n).start()

        halves(bits(s)[1], add)

    for s in range(D):
        @pl.when(d == s)
        def _(s=s):
            b, e, partner, across = bits(s)

            def piece(fb, lo, n):
                return fin.at[pl.ds(pl.multiple_of((2 * fb + bc) * Q + lo, 16), n)]

            def share(k, fb, lo, n, target):
                return copy(piece(fb, lo, n), piece(fb, lo, n), s5.at[k], q5.at[k], target)

            targets = (partner, across, pxy)

            def finish(lo, n, olo, on):
                at = pl.ds(lo, n)
                total = a3[s, at].astype(f32)
                for t in range(1, D):
                    stage4(s, t, lo, n).wait_recv()
                    total = total + r4[t - 1, at].astype(f32)
                piece(b, lo, n)[...] = total.astype(bf16)
                for k in range(3):
                    share(k, b, lo, n, targets[k]).start()
                share(0, 1 - b, lo, n, partner).wait_recv()
                share(1, b, olo, on, across).wait_recv()
                share(2, 1 - b, olo, on, pxy).wait_recv()

            halves(e, finish)

    def stage6(b, c):
        ref = fin.at[pl.ds(pl.multiple_of((2 * b + c) * Q, 16), Q)]
        return copy(ref, ref, s6.at[b], q6.at[b], pc)

    for b in range(2):
        stage6(b, bc).start()
    for b in range(2):
        stage6(b, 1 - bc).wait_recv()
    out[...] = fin[...]

    for s in range(D):
        for b in range(2):
            stage1(s, b).wait_send()
        stage2(s).wait_send()

        def drain(lo, n, olo, on, s=s):
            stage3(s, olo, on).wait_send()
            for t in range(1, D):
                @pl.when(lax.rem(d + t, D) == s)
                def _(t=t):
                    stage4(s, t, lo, n).wait_send()

            @pl.when(d == s)
            def _():
                for k in range(3):
                    ref = fin.at[pl.ds(lo, n)]
                    copy(ref, ref, s5.at[k], q5.at[k], pc).wait_send()

        halves(bits(s)[1], drain)
    for b in range(2):
        stage6(b, bc).wait_send()


def adam_update(master, moment_one, moment_two, gradient):
    new_one = beta_one * moment_one + (1.0 - beta_one) * gradient
    new_two = beta_two * moment_two + (1.0 - beta_two) * gradient * gradient
    update = new_one / (1.0 - beta_one**10) / (jnp.sqrt(new_two / (1.0 - beta_two**10)) + epsilon)
    return (master - learn_rate * update, new_one, new_two)


def per_device(counts, volume, cotangent, master, moment_one, moment_two):
    D, GX, GY = counts
    _, sx, sy, sz, width = volume.shape
    ry = sy * sz
    H = master.shape[0]
    Q = H // 4
    sem = pltpu.SemaphoreType.DMA
    whole = pl.BlockSpec(memory_space=VMEM)
    vol = volume.reshape(sx, ry, width)
    cot = cotangent.reshape(sx, ry, width)
    vext, cext, w = pl.pallas_call(
        functools.partial(gather_kernel, counts),
        out_shape=(
            jax.ShapeDtypeStruct((sx + 2 * HX, ry + 16 * HY, width), bf16),
            jax.ShapeDtypeStruct((sx + 2, ry + 16 * CY, width), bf16),
            jax.ShapeDtypeStruct((D * H, width), bf16),
        ),
        in_specs=[whole] * 3,
        out_specs=(whole,) * 3,
        scratch_shapes=[sem((2, 8)), sem((2, 8)), sem((5, D)), sem((5, D))],
        compiler_params=pltpu.CompilerParams(
            collective_id=0, has_side_effects=True, vmem_limit_bytes=24 * 2**20
        ),
        name="gather",
    )(vol, cot, master)
    n1, n2 = ry + 32, ry + 16
    act, grad = pl.pallas_call(
        functools.partial(compute_kernel, counts),
        out_shape=(
            jax.ShapeDtypeStruct((sx, ry, width), bf16),
            jax.ShapeDtypeStruct((D * H, width), bf16),
        ),
        in_specs=[whole] * 3,
        out_specs=(whole,) * 2,
        scratch_shapes=[
            VMEM((sx + 6, n1, 9 * C), bf16),
            VMEM((sx + 4, n2, 9 * C), bf16),
            VMEM((sx + 2, ry, 9 * C), bf16),
            VMEM((sx + 4, n1, C), f32),
            VMEM((3, C, 9 * C), bf16),
            VMEM((sx + 2, n1, 3 * C), bf16),
            VMEM((sx + 2, n2, 3 * C), bf16),
        ],
        compiler_params=pltpu.CompilerParams(vmem_limit_bytes=48 * 2**20),
        name="compute",
    )(vext, cext, w)
    rows = pl.pallas_call(
        functools.partial(reduce_kernel, counts),
        out_shape=jax.ShapeDtypeStruct((H, width), bf16),
        in_specs=[whole],
        out_specs=whole,
        scratch_shapes=[
            VMEM((D, 2, Q, width), bf16),
            VMEM((D, 2, Q, width), bf16),
            VMEM((D, Q, width), bf16),
            VMEM((D, Q, width), bf16),
            VMEM((D, Q, width), bf16),
            VMEM((D, Q, width), bf16),
            VMEM((D - 1, Q, width), bf16),
            VMEM((H, width), bf16),
            sem((D, 2)), sem((D, 2)), sem((D,)), sem((D,)), sem((D,)), sem((D,)),
            sem((D - 1,)), sem((D - 1,)), sem((3,)), sem((3,)), sem((2,)), sem((2,)),
        ],
        compiler_params=pltpu.CompilerParams(
            collective_id=1, has_side_effects=True, vmem_limit_bytes=24 * 2**20
        ),
        name="reduce",
    )(grad)
    new_master, new_one, new_two = adam_update(master, moment_one, moment_two, rows.astype(f32))
    return (act.reshape(volume.shape), new_master, new_one, new_two)


def solution(mesh):
    counts = (mesh.shape["dp"], mesh.shape["gx"], mesh.shape["gy"])
    return jax.shard_map(
        functools.partial(per_device, counts),
        mesh=mesh,
        in_specs=(
            P("dp", "gx", "gy", None, None),
            P("dp", "gx", "gy", None, None),
            P("dp", None),
            P("dp", None),
            P("dp", None),
        ),
        out_specs=(P("dp", "gx", "gy", None, None), P("dp", None), P("dp", None), P("dp", None)),
        check_vma=False,
    )
```

time: 244 us -> 62.8 us (0.26)
  waiting for transfers between devices: 74.4 us -> 0 us
  blocking collectives: 74.1 us -> 0 us
  Pallas kernels: 0 us -> 57 us
  matrix products: 32.8 us -> 0 us
  starting transfers between devices: 31.8 us -> 0 us
  between operations: 16.2 us -> 0.7 us
  other arithmetic: 10.4 us -> 1.87 us
    psum x1 -> x0, blocking collectives: 74.1 us -> none  [per_device(): summed = lax.psum(gradient, ('gx', 'gy'))]
    pallas_call x0 -> x3, Pallas kernels: none -> 57 us  [the longest x1 23.2 us: per_device(): pl.pallas_call(functools.partial(reduce_kernel, counts), out_shape=jax.Sh...]
    reduce_scatter x1 -> x0, waiting for transfers between devices: 36.4 us -> none  [per_device(): lax.psum_scatter(summed.astype(jnp.bfloat16), 'dp', scatter_dimension=0,...]
    dot_general x135 -> x0, matrix products: 32.8 us -> none  [the longest x81 20.5 us: convolve(): jnp.dot(window.reshape(-1, padded.shape[3]), kernel[9 * offset_x + 3 * of...]
    ppermute x12 -> x0, starting transfers between devices: 31.8 us -> none  [the longest x6 21.9 us: extended(): lax.ppermute(tail, axis, [(i, (i + 1) % count) for i in range(ends)])]
    all_gather x1 -> x0, waiting for transfers between devices: 19.7 us -> none  [per_device(): full_weights = lax.all_gather(local_weights, 'dp', axis=0, tiled=True)]
    ppermute x12 -> x0, waiting for transfers between devices: 18.3 us -> none  [the longest x6 18.3 us: extended(): lax.ppermute(head, axis, [((i + 1) % count, i) for i in range(ends)])]
    concatenate x9 -> x0, other arithmetic: 3.93 us -> none  [extended(): jnp.concatenate([lax.ppermute(tail, axis, [(i, (i + 1) % count) for i in...]
  transfers between devices with their start and end apart: 14 -> 0, of which waited for: 8 -> 0; matrix products, arithmetic and copies ran while one was open for 2% -> 0% of each run, Pallas kernels for 0% -> 0%
where the time goes in v1:
time: 62.8 us; the launch traced here: 62.6 us
  Pallas kernels  57 us (91%)
  local copies, waits for them, and re-layouts  2.99 us (5%)
  other arithmetic  1.87 us (3%)
  between operations  0.7 us (1%)
    pallas_call x1, Pallas kernels, per_device(): pl.pallas_call(functools.partial(reduce_kernel, counts), out_shape=jax.Sh...  23.2 us
    pallas_call x1, Pallas kernels, per_device(): pl.pallas_call(functools.partial(gather_kernel, counts), out_shape=(jax.S...  22.5 us
    pallas_call x1, Pallas kernels, per_device(): pl.pallas_call(functools.partial(compute_kernel, counts), out_shape=(jax....  11.3 us
    unnamed x12, local copies, waits for them, and re-layouts  2.99 us
    sub x1, other arithmetic, adam_update(): return (master - learn_rate * update, new_one, new_two)  1.87 us

profile of v1, /device:TPU:1, one launch (start us, length us, event | category | flops | bytes accessed | tf_op | source)
XLA Modules:
  0.0 62.6 jit_solution(8867670549891349095)
XLA Ops:
  0.6 0.0 copy-start
  0.6 1.2 %copy-done = f32[1728,128]{1,0:T(8,128)S(1)} copy-done((f32[1728,128]{1,0:T(8,128)S(1)}, f32[1728,128]{1,0:T(8,128)}, u32[]{:S(2)}) %copy-start) | copy-done | bytes 884760
  1.8 0.0 copy-start.2
  1.8 0.9 %copy-done.2 = bf16[1,4,16,8,128]{4,3,2,1,0:T(8,128)(2,1)S(1)} copy-done((bf16[1,4,16,8,128]{4,3,2,1,0:T(8,128)(2,1)S(1)}, bf16[1,4,16,8,128]{4,3,2,1,0:T(8,128)(2,1)}, u32[]{:S(2)}) %copy-start.2) | copy-done | bytes 131096
  2.7 0.0 copy-start.3
  2.7 0.9 %copy-done.3 = bf16[1,4,16,8,128]{4,3,2,1,0:T(8,128)(2,1)S(1)} copy-done((bf16[1,4,16,8,128]{4,3,2,1,0:T(8,128)(2,1)S(1)}, bf16[1,4,16,8,128]{4,3,2,1,0:T(8,128)(2,1)}, u32[]{:S(2)}) %copy-start.3) | copy-done | bytes 131096
  3.6 22.5 %gather.1 = (bf16[10,192,128]{2,1,0:T(8,128)(2,1)S(1)}, bf16[6,160,128]{2,1,0:T(8,128)(2,1)S(1)}, bf16[6912,128]{1,0:T(8,128)(2,1)S(1)}) custom-call(bf16[4,128,128]{2,1,0:T(8,128)(2,1)S(1)} %bitcast.3, bf16[4,128,128]{2,1,0:T(8,128)(2,1)S(1)} %bitcast.4, f32[1728,128]{1,0:T(8,128)S(1)} %copy-done), custom_call_target="tpu_custom_call" | custom-call | tf_op jit(solution)/shard_map/gather/pallas_call | solution.py:502
  26.1 0.0 copy-start.1
  26.1 0.0 copy-start.4
  26.1 0.0 copy-start.5
  26.2 11.3 %compute.1 = (bf16[4,128,128]{2,1,0:T(8,128)(2,1)}, bf16[6912,128]{1,0:T(8,128)(2,1)S(1)}) custom-call(bf16[10,192,128]{2,1,0:T(8,128)(2,1)S(1)} %get-tuple-element.9.vext, bf16[6,160,128]{2,1,0:T(8,128)(2,1)S(1)} %get-tuple-element.10.cext, bf16[6912,128]{1,0:T(8,128)(2,1)S(1)} %get-tuple-element.11.w), custom_call_target="tpu_custom_call" | custom-call | tf_op jit(solution)/shard_map/compute/pallas_call | solution.py:518
  37.4 23.2 %reduce.1 = bf16[1728,128]{1,0:T(8,128)(2,1)S(1)} custom-call(bf16[6912,128]{1,0:T(8,128)(2,1)S(1)} %get-tuple-element.13.g), custom_call_target="tpu_custom_call" | custom-call | tf_op jit(solution)/shard_map/reduce/pallas_call | solution.py:538
  60.7 0.0 copy-done.1
  60.7 0.0 copy-done.4
  60.7 0.0 copy-done.5
  60.7 1.9 %multiply_subtract_fusion = (f32[1728,128]{1,0:T(8,128)}, f32[1728,128]{1,0:T(8,128)}, f32[1728,128]{1,0:T(8,128)}) fusion(f32[1728,128]{1,0:T(8,128)S(1)} %copy-done.1, bf16[1728,128]{1,0:T(8,128)(2,1)S(1)} %reduce.1, f32[1728,128]{1,0:T(8,128)S(1)} %copy-done.4, f32[1728,128]{1,0:T(8,128)S(1)} %copy-done.5), kind=kLoop, calls=%fused_computation.4 | loop fusion | flops 3096576 | bytes 5750784 | tf_op jit(solution)/shard_map/sub | solution.py:489
Async XLA Ops:
  0.6 1.2 %copy-start = (f32[1728,128]{1,0:T(8,128)S(1)}, f32[1728,128]{1,0:T(8,128)}, u32[]{:S(2)}) copy-start(f32[1728,128]{1,0:T(8,128)} %master.1) | copy-start | bytes 2654212
  1.8 0.9 %copy-start.2 = (bf16[1,4,16,8,128]{4,3,2,1,0:T(8,128)(2,1)S(1)}, bf16[1,4,16,8,128]{4,3,2,1,0:T(8,128)(2,1)}, u32[]{:S(2)}) copy-start(bf16[1,4,16,8,128]{4,3,2,1,0:T(8,128)(2,1)} %param.5) | copy-start | bytes 393220
  2.7 0.9 %copy-start.3 = (bf16[1,4,16,8,128]{4,3,2,1,0:T(8,128)(2,1)S(1)}, bf16[1,4,16,8,128]{4,3,2,1,0:T(8,128)(2,1)}, u32[]{:S(2)}) copy-start(bf16[1,4,16,8,128]{4,3,2,1,0:T(8,128)(2,1)} %param.6) | copy-start | bytes 393220
  26.1 34.6 %copy-start.1 = (f32[1728,128]{1,0:T(8,128)S(1)}, f32[1728,128]{1,0:T(8,128)}, u32[]{:S(2)}) copy-start(f32[1728,128]{1,0:T(8,128)} %master.1) | copy-start | bytes 2654212
  26.1 34.6 %copy-start.4 = (f32[1728,128]{1,0:T(8,128)S(1)}, f32[1728,128]{1,0:T(8,128)}, u32[]{:S(2)}) copy-start(f32[1728,128]{1,0:T(8,128)} %param.8) | copy-start | bytes 2654212
  26.1 34.6 %copy-start.5 = (f32[1728,128]{1,0:T(8,128)S(1)}, f32[1728,128]{1,0:T(8,128)}, u32[]{:S(2)}) copy-start(f32[1728,128]{1,0:T(8,128)} %param.9) | copy-start | bytes 2654212

commit v2 on v1

--- a/solution.py
+++ b/solution.py
@@ -38,12 +38,16 @@
     return index + step - 2 * step * bit
 
 
-def gather_kernel(counts, vol, cot, master, vext, cext, w, hsend, hrecv, wsend, wrecv):
+def gather_phases(counts, vol, cot, master_hbm, master, vext, cext, w, msem, hsend, hrecv, wsend, wrecv):
     D, GX, GY = counts
     d, x, y, bx, by, bc = place()
     sx, ry = vol.shape[0], vol.shape[1]
     H = master.shape[0]
     Q = H // 4
+    N = 3
+    part_rows = Q // N
+    load = pltpu.make_async_copy(master_hbm, master, msem)
+    load.start()
     here = {"x": (d, flip(x, bx, 1), y), "y": (d, x, flip(y, by, 2)), "c": (d, x, flip(y, bc, 1))}
 
     vext[...] = jnp.zeros_like(vext)
@@ -59,9 +63,9 @@
         return ok
 
     barrier = pltpu.get_barrier_semaphore()
-    total = jnp.int32(3)
-    for key in ("x", "y", "c"):
-        pl.semaphore_signal(barrier, inc=1, device_id=here[key], device_id_type=MESH)
+    total = jnp.int32(4)
+    for target in (here["x"], here["y"], here["c"], (d, here["x"][1], here["y"][2])):
+        pl.semaphore_signal(barrier, inc=1, device_id=target, device_id_type=MESH)
     for i, j in around:
         ok = exists(i, j)
 
@@ -70,60 +74,57 @@
             pl.semaphore_signal(barrier, inc=1, device_id=(d, x + i, y + j), device_id_type=MESH)
 
         total = total + jnp.where(ok, 1, 0)
-    for step in (-1, 1):
-        ok = (d + step >= 0) & (d + step < D)
-
-        @pl.when(ok)
-        def _(step=step):
-            pl.semaphore_signal(barrier, inc=1, device_id=(d + step, x, y), device_id_type=MESH)
-
-        total = total + jnp.where(ok, 1, 0)
+    for t in range(1, D):
+        pl.semaphore_signal(barrier, inc=1, device_id=(lax.rem(d + t, D), x, y), device_id_type=MESH)
+    total = total + (D - 1)
 
     vext[pl.ds(HX, sx), pl.ds(8 * HY, ry)] = vol[...]
     cext[pl.ds(1, sx), pl.ds(8 * CY, ry)] = cot[...]
+    load.wait()
     w[pl.ds(pl.multiple_of(d * H, 16), H)] = master[...].astype(bf16)
     pl.semaphore_wait(barrier, total)
 
-    def rows(s, q):
-        return w.at[pl.ds(pl.multiple_of(s * H + q * Q, 16), Q)]
-
-    def move(ref, k, s, target):
+    def rows(s, q, n):
+        return w.at[pl.ds(pl.multiple_of(s * H + q * Q + n * part_rows, 16), part_rows)]
+
+    def move(ref, k, s, n, target):
         return pltpu.make_async_remote_copy(
-            src_ref=ref, dst_ref=ref, send_sem=wsend.at[k, s], recv_sem=wrecv.at[k, s],
+            src_ref=ref, dst_ref=ref, send_sem=wsend.at[k, s, n], recv_sem=wrecv.at[k, s, n],
             device_id=target, device_id_type=MESH,
         )
 
     def bit(s):
-        even = lax.rem(s, 2) == 0
-        return even, jnp.where(even, bx, by)
+        return jnp.where(lax.rem(s, 2) == 0, bx, by)
 
     def quarter(s):
-        return 2 * bit(s)[1] + bc
+        return 2 * bit(s) + bc
 
     def other(s):
-        return 2 * (1 - bit(s)[1]) + bc
-
-    def up(s):
-        return move(rows(s, quarter(s)), 0, s, (d + 1, x, y))
-
-    def down(s):
-        return move(rows(s, quarter(s)), 1, s, (d - 1, x, y))
-
-    def partner(s, q):
+        return 2 * (1 - bit(s)) + bc
+
+    def up(s, n):
+        return move(rows(s, quarter(s), n), 0, s, n, (d + 1, x, y))
+
+    def down(s, n):
+        return move(rows(s, quarter(s), n), 1, s, n, (d - 1, x, y))
+
+    def partner(s, q, n):
         even = lax.rem(s, 2) == 0
         target = (d, jnp.where(even, here["x"][1], x), jnp.where(even, y, here["y"][2]))
-        return move(rows(s, q), 2, s, target)
-
-    def sibling(s, q, k):
-        return move(rows(s, q), k, s, here["c"])
+        return move(rows(s, q, n), 2, s, n, target)
+
+    def sibling(s, q, k, n):
+        return move(rows(s, q, n), k, s, n, here["c"])
 
     @pl.when(d < D - 1)
     def _():
-        up(d).start()
+        for n in range(N):
+            up(d, n).start()
 
     @pl.when(d > 0)
     def _():
-        down(d).start()
+        for n in range(N):
+            down(d, n).start()
 
     def halo(n, i, j):
         def part(step, halo_x, size):
@@ -153,83 +154,87 @@
             for copy in halo(n, i, j):
                 copy.start()
 
-    def spread(s):
-        partner(s, quarter(s)).start()
-        sibling(s, quarter(s), 3).start()
-
-    def pass_on(s):
-        partner(s, other(s)).wait_recv()
-        sibling(s, other(s), 4).start()
-
-    for t in range(1, D):
-        @pl.when(d - t >= 0)
-        def _(t=t):
-            s = d - t
-            up(s).wait_recv()
-
-            @pl.when(d < D - 1)
-            def _():
-                up(s).start()
-
-            spread(s)
-
-        @pl.when(d + t < D)
-        def _(t=t):
-            s = d + t
-            down(s).wait_recv()
-
-            @pl.when(d > 0)
-            def _():
-                down(s).start()
-
-            spread(s)
-
-        if t > 1:
-            @pl.when(d - t + 1 >= 0)
-            def _(t=t):
-                pass_on(d - t + 1)
-
-            @pl.when(d + t - 1 < D)
-            def _(t=t):
-                pass_on(d + t - 1)
-
-    @pl.when(d - D + 1 >= 0)
-    def _():
-        pass_on(d - D + 1)
-
-    @pl.when(d + D - 1 < D)
-    def _():
-        pass_on(d + D - 1)
-
-    for t in range(1, D):
-        for sign in (-1, 1):
+    def relay(t, n):
+        for sign, line, more in ((-1, up, d < D - 1), (1, down, d > 0)):
             s = d + sign * t
 
+            @pl.when((s >= 0) & (s < D))
+            def _(s=s, line=line, more=more):
+                line(s, n).wait_recv()
+
+                @pl.when(more)
+                def _():
+                    line(s, n).start()
+
+                partner(s, quarter(s), n).start()
+                sibling(s, quarter(s), 3, n).start()
+
+    def pass_on(t, n):
+        for s in (d - t, d + t):
             @pl.when((s >= 0) & (s < D))
             def _(s=s):
-                theirs = 2 * bit(s)[1] + 1 - bc
-                sibling(s, theirs, 3).wait_recv()
-                sibling(s, 2 * (1 - bit(s)[1]) + 1 - bc, 4).wait_recv()
-                partner(s, quarter(s)).wait_send()
-                sibling(s, quarter(s), 3).wait_send()
-                sibling(s, other(s), 4).wait_send()
+                partner(s, other(s), n).wait_recv()
+                sibling(s, other(s), 4, n).start()
+
+    for n in range(N):
+        relay(1, n)
+
+    for n, (i, j) in enumerate(around):
+        @pl.when(exists(i, j))
+        def _(n=n, i=i, j=j):
+            for copy in halo(7 - n, -i, -j):
+                copy.wait_recv()
+
+    yield
+
+    steps = [(t, n) for t in range(1, D) for n in range(N)]
+    behind = 0
+    for at in range(N, len(steps)):
+        relay(*steps[at])
+        if at >= N:
+            pass_on(*steps[behind])
+            behind += 1
+    for at in range(behind, len(steps)):
+        pass_on(*steps[at])
+
+    for low, high in ((0, D // 2), (D // 2, D)):
+        for s in range(low, high):
+            @pl.when(d != s)
+            def _(s=s):
+                z = jnp.int32(s)
+                for n in range(N):
+                    sibling(z, 2 * bit(z) + 1 - bc, 3, n).wait_recv()
+                    sibling(z, 2 * (1 - bit(z)) + 1 - bc, 4, n).wait_recv()
+
+        yield
 
     for s in range(D):
+        z = jnp.int32(s)
+
+        @pl.when(d != s)
+        def _(z=z):
+            for n in range(N):
+                partner(z, quarter(z), n).wait_send()
+                sibling(z, quarter(z), 3, n).wait_send()
+                sibling(z, other(z), 4, n).wait_send()
+
         @pl.when((s <= d) & (d < D - 1))
-        def _(s=s):
-            up(jnp.int32(s)).wait_send()
+        def _(z=z):
+            for n in range(N):
+                up(z, n).wait_send()
 
         @pl.when((s >= d) & (d > 0))
-        def _(s=s):
-            down(jnp.int32(s)).wait_send()
+        def _(z=z):
+            for n in range(N):
+                down(z, n).wait_send()
 
     for n, (i, j) in enumerate(around):
         @pl.when(exists(i, j))
         def _(n=n, i=i, j=j):
             for copy in halo(n, i, j):
                 copy.wait_send()
-            for copy in halo(7 - n, -i, -j):
-                copy.wait_recv()
+
+    yield
 
 
 def shifted(field):
@@ -248,7 +253,7 @@
             out[:, k * C : (k + 1) * C] = views[c][first + 8 * b : first + 8 * b + rows].astype(bf16)
 
 
-def compute_kernel(counts, vext, cext, w, act, grad, x1, x2, x3, first, kt, d1, d2):
+def compute_phases(counts, vext, cext, w, act, grad, x1, x2, x3, first, kt, d1, d2):
     D, GX, GY = counts
     sx = vext.shape[0] - 2 * HX
     ry = vext.shape[1] - 16 * HY
@@ -263,10 +268,7 @@
     def _(s):
         unfold(vext[s].astype(f32), 8, n1, x1.at[s])
 
-    for a in range(3):
-        for k in range(9):
-            base = (27 + 9 * (2 - a) + 8 - k) * C
-            kt[a, :, k * C : (k + 1) * C] = w[base : base + C]
+    yield
 
     def conv(source, kernel, at, size, contract):
         total = None
@@ -296,6 +298,13 @@
             hidden = gelu_value(piece).astype(bf16).astype(f32) * (y_ok * x_ok)
             unfold(hidden, 0, n2, x2.at[s])
 
+    yield
+
+    for a in range(3):
+        for k in range(9):
+            base = (27 + 9 * (2 - a) + 8 - k) * C
+            kt[a, :, k * C : (k + 1) * C] = w[base : base + C]
+
     half2 = (sx + 2) // 2
 
     @pl.loop(0, 2)
@@ -330,6 +339,7 @@
                 grad[pl.ds(at, 3 * C)] = out[:, a * C : (a + 1) * C].astype(bf16)
 
     weight_grad(x2, 1, d2, 27 * C)
+    yield
 
     back = conv(x3, lambda a: kt[a], 0, sx, 1)
     for i in range(sx):
@@ -338,10 +348,13 @@
         delta = (piece * slope).astype(bf16)
         for a in range(3):
             d1[i + a, 16 : 16 + ry, a * C : (a + 1) * C] = delta
+    yield
+
     weight_grad(x1, 2, d1, 0)
-
-
-def reduce_kernel(counts, g, out, r1, a1, r2, a2, r3, a3, r4, fin, s1, q1, s2, q2, s3, q3, s4, q4, s5, q5, s6, q6):
+    yield
+
+
+def reduce_phases(counts, g, out, r1, a1, r2, a2, r3, a3, r4, fin, s1, q1, s2, q2, s3, q3, s4, q4, s5, q5, s6, q6):
     D, GX, GY = counts
     d, x, y, bx, by, bc = place()
     H = out.shape[0]
@@ -350,13 +363,6 @@
     px, py, pc = (d, flip(x, bx, 1), y), (d, x, flip(y, by, 2)), (d, x, flip(y, bc, 1))
     pxy = (d, flip(x, bx, 1), flip(y, by, 2))
 
-    barrier = pltpu.get_barrier_semaphore()
-    for target in (px, py, pc, pxy):
-        pl.semaphore_signal(barrier, inc=1, device_id=target, device_id_type=MESH)
-    for t in range(1, D):
-        pl.semaphore_signal(barrier, inc=1, device_id=(lax.rem(d + t, D), x, y), device_id_type=MESH)
-    pl.semaphore_wait(barrier, 4 + D - 1)
-
     def copy(src, dst, send, recv, target):
         return pltpu.make_async_remote_copy(
             src_ref=src, dst_ref=dst, send_sem=send, recv_sem=recv, device_id=target, device_id_type=MESH
@@ -388,29 +394,27 @@
         target = bits(s)[3]
         return copy(a2.at[s, pl.ds(lo, n)], r3.at[s, pl.ds(lo, n)], s3.at[s], q3.at[s], target)
 
-    for s in range(D):
+    def begin(s):
         for b in range(2):
             stage1(s, b).start()
-    for s in range(D):
+
+    def after1(s):
         for b in range(2):
             stage1(s, b).wait_recv()
             a1[s, b] = (g[quarter(s, 2 * b + bc)].astype(f32) + r1[s, b].astype(f32)).astype(bf16)
         stage2(s).start()
-    for s in range(D):
+
+    def after2(s):
         stage2(s).wait_recv()
         b = bits(s)[0]
         a2[s] = (a1[s, b].astype(f32) + r2[s].astype(f32)).astype(bf16)
-
-        def send(lo, n, olo, on, s=s):
-            stage3(s, olo, on).start()
-
-        halves(bits(s)[1], send)
+        halves(bits(s)[1], lambda lo, n, olo, on: stage3(s, olo, on).start())
 
     def stage4(s, t, lo, n):
         return copy(a3.at[s, pl.ds(lo, n)], r4.at[t - 1, pl.ds(lo, n)], s4.at[t - 1], q4.at[t - 1], (s, x, y))
 
-    for s in range(D):
-        def add(lo, n, olo, on, s=s):
+    def after3(s):
+        def add(lo, n, olo, on):
             stage3(s, lo, n).wait_recv()
             at = pl.ds(lo, n)
             a3[s, at] = (a2[s, at].astype(f32) + r3[s, at].astype(f32)).astype(bf16)
@@ -420,6 +424,26 @@
                     stage4(s, t, lo, n).start()
 
         halves(bits(s)[1], add)
+
+    early, late = range(D // 2, D), range(D // 2)
+    for s in early:
+        begin(s)
+    yield
+    for s in early:
+        after1(s)
+    yield
+    for s in late:
+        begin(s)
+    for s in early:
+        after2(s)
+    for s in late:
+        after1(s)
+    for s in early:
+        after3(s)
+    for s in late:
+        after2(s)
+    for s in late:
+        after3(s)
 
     for s in range(D):
         @pl.when(d == s)
@@ -480,6 +504,26 @@
         halves(bits(s)[1], drain)
     for b in range(2):
         stage6(b, bc).wait_send()
+    yield
+
+
+def step_kernel(counts, vol, cot, master_hbm, act, out, master, vext, cext, w, g, *scratch):
+    msem, moves, fields, sums = scratch[0], scratch[1:5], scratch[5:12], scratch[12:]
+    gather = gather_phases(counts, vol, cot, master_hbm, master, vext, cext, w, msem, *moves)
+    compute = compute_phases(counts, vext, cext, w, act, g, *fields)
+    reduce = reduce_phases(counts, g, out, *sums)
+    next(gather)
+    next(compute)
+    next(gather)
+    next(compute)
+    next(gather)
+    next(compute)
+    next(reduce)
+    next(compute)
+    next(reduce)
+    next(compute)
+    next(reduce)
+    next(gather)
 
 
 def adam_update(master, moment_one, moment_two, gradient):
@@ -499,31 +543,22 @@
     whole = pl.BlockSpec(memory_space=VMEM)
     vol = volume.reshape(sx, ry, width)
     cot = cotangent.reshape(sx, ry, width)
-    vext, cext, w = pl.pallas_call(
-        functools.partial(gather_kernel, counts),
-        out_shape=(
-            jax.ShapeDtypeStruct((sx + 2 * HX, ry + 16 * HY, width), bf16),
-            jax.ShapeDtypeStruct((sx + 2, ry + 16 * CY, width), bf16),
-            jax.ShapeDtypeStruct((D * H, width), bf16),
-        ),
-        in_specs=[whole] * 3,
-        out_specs=(whole,) * 3,
-        scratch_shapes=[sem((2, 8)), sem((2, 8)), sem((5, D)), sem((5, D))],
-        compiler_params=pltpu.CompilerParams(
-            collective_id=0, has_side_effects=True, vmem_limit_bytes=24 * 2**20
-        ),
-        name="gather",
-    )(vol, cot, master)
     n1, n2 = ry + 32, ry + 16
-    act, grad = pl.pallas_call(
-        functools.partial(compute_kernel, counts),
+    act, rows = pl.pallas_call(
+        functools.partial(step_kernel, counts),
         out_shape=(
             jax.ShapeDtypeStruct((sx, ry, width), bf16),
-            jax.ShapeDtypeStruct((D * H, width), bf16),
+            jax.ShapeDtypeStruct((H, width), bf16),
         ),
-        in_specs=[whole] * 3,
+        in_specs=[whole, whole, pl.BlockSpec(memory_space=pl.ANY)],
         out_specs=(whole,) * 2,
         scratch_shapes=[
+            VMEM((H, width), f32),
+            VMEM((sx + 2 * HX, ry + 16 * HY, width), bf16),
+            VMEM((sx + 2, ry + 16 * CY, width), bf16),
+            VMEM((D * H, width), bf16),
+            VMEM((D * H, width), bf16),
+            sem(()), sem((2, 8)), sem((2, 8)), sem((5, D, 3)), sem((5, D, 3)),
             VMEM((sx + 6, n1, 9 * C), bf16),
             VMEM((sx + 4, n2, 9 * C), bf16),
             VMEM((sx + 2, ry, 9 * C), bf16),
@@ -531,16 +566,6 @@
             VMEM((3, C, 9 * C), bf16),
             VMEM((sx + 2, n1, 3 * C), bf16),
             VMEM((sx + 2, n2, 3 * C), bf16),
-        ],
-        compiler_params=pltpu.CompilerParams(vmem_limit_bytes=48 * 2**20),
-        name="compute",
-    )(vext, cext, w)
-    rows = pl.pallas_call(
-        functools.partial(reduce_kernel, counts),
-        out_shape=jax.ShapeDtypeStruct((H, width), bf16),
-        in_specs=[whole],
-        out_specs=whole,
-        scratch_shapes=[
             VMEM((D, 2, Q, width), bf16),
             VMEM((D, 2, Q, width), bf16),
             VMEM((D, Q, width), bf16),
@@ -553,10 +578,11 @@
             sem((D - 1,)), sem((D - 1,)), sem((3,)), sem((3,)), sem((2,)), sem((2,)),
         ],
         compiler_params=pltpu.CompilerParams(
-            collective_id=1, has_side_effects=True, vmem_limit_bytes=24 * 2**20
+            collective_id=0, has_side_effects=True, vmem_limit_bytes=44 * 2**20
         ),
-        name="reduce",
-    )(grad)
+        cost_estimate=pl.CostEstimate(flops=4 * 10**10, bytes_accessed=10**8, transcendentals=10**6),
+        name="step",
+    )(vol, cot, master)
     new_master, new_one, new_two = adam_update(master, moment_one, moment_two, rows.astype(f32))
     return (act.reshape(volume.shape), new_master, new_one, new_two)
 

time: 62.8 us -> 59.4 us (0.946)
  Pallas kernels: 57 us -> 53.1 us
  local copies, waits for them, and re-layouts: 2.99 us -> 3.63 us
    pallas_call x3 -> x1, Pallas kernels: 57 us -> 53.1 us  [per_device(): pl.pallas_call(functools.partial(step_kernel, counts), out_shape=(jax.Sha...]
    unnamed x12 -> x11, local copies, waits for them, and re-layouts: 2.99 us -> 3.63 us
where the time goes in v2:
time: 59.4 us; the launch traced here: 59.2 us
  Pallas kernels  53.1 us (89%)
  local copies, waits for them, and re-layouts  3.63 us (6%)
  other arithmetic  1.87 us (3%)
  between operations  0.67 us (1%)
    pallas_call x1, Pallas kernels, per_device(): pl.pallas_call(functools.partial(step_kernel, counts), out_shape=(jax.Sha...  53.1 us
    unnamed x11, local copies, waits for them, and re-layouts  3.63 us
    sub x1, other arithmetic, adam_update(): return (master - learn_rate * update, new_one, new_two)  1.87 us

profile of v2, /device:TPU:1, one launch (start us, length us, event | category | flops | bytes accessed | tf_op | source)
XLA Modules:
  0.0 59.2 jit_solution(7497638208923865774)
XLA Ops:
  0.6 0.0 copy-start
  0.6 1.2 %copy-done = f32[1728,128]{1,0:T(8,128)S(1)} copy-done((f32[1728,128]{1,0:T(8,128)S(1)}, f32[1728,128]{1,0:T(8,128)}, u32[]{:S(2)}) %copy-start) | copy-done | bytes 884760
  1.8 0.0 copy-start.1
  1.8 0.9 %copy-done.1 = bf16[1,4,16,8,128]{4,3,2,1,0:T(8,128)(2,1)S(1)} copy-done((bf16[1,4,16,8,128]{4,3,2,1,0:T(8,128)(2,1)S(1)}, bf16[1,4,16,8,128]{4,3,2,1,0:T(8,128)(2,1)}, u32[]{:S(2)}) %copy-start.1) | copy-done | bytes 131096
  2.7 0.0 copy-start.2
  2.7 0.9 %copy-done.2 = bf16[1,4,16,8,128]{4,3,2,1,0:T(8,128)(2,1)S(1)} copy-done((bf16[1,4,16,8,128]{4,3,2,1,0:T(8,128)(2,1)S(1)}, bf16[1,4,16,8,128]{4,3,2,1,0:T(8,128)(2,1)}, u32[]{:S(2)}) %copy-start.2) | copy-done | bytes 131096
  3.6 0.0 copy-start.3
  3.6 0.0 copy-start.4
  3.6 53.1 %step.1 = (bf16[4,128,128]{2,1,0:T(8,128)(2,1)S(1)}, bf16[1728,128]{1,0:T(8,128)(2,1)S(1)}) custom-call(bf16[4,128,128]{2,1,0:T(8,128)(2,1)S(1)} %bitcast.4, bf16[4,128,128]{2,1,0:T(8,128)(2,1)S(1)} %bitcast.5, f32[1728,128]{1,0:T(8,128)S(1)} %copy-done), custom_call_target="tpu_custom_call" | custom-call | flops 40000000000 | bytes 100000000 | tf_op jit(solution)/shard_map/step/pallas_call | solution.py:547
  56.7 0.0 copy-done.3
  56.7 0.0 copy-done.4
  56.7 1.9 %multiply_subtract_fusion = (f32[1728,128]{1,0:T(8,128)}, f32[1728,128]{1,0:T(8,128)}, f32[1728,128]{1,0:T(8,128)}) fusion(f32[1728,128]{1,0:T(8,128)S(1)} %copy-done, bf16[1728,128]{1,0:T(8,128)(2,1)S(1)} %get-tuple-element.7, f32[1728,128]{1,0:T(8,128)S(1)} %copy-done.3, f32[1728,128]{1,0:T(8,128)S(1)} %copy-done.4), kind=kLoop, calls=%fused_computation.4 | loop fusion | flops 3096576 | bytes 5750784 | tf_op jit(solution)/shard_map/sub | solution.py:533
  58.6 0.7 %copy.10 = bf16[1,4,16,8,128]{4,3,2,1,0:T(8,128)(2,1)} copy(bf16[1,4,16,8,128]{4,3,2,1,0:T(8,128)(2,1)S(1)} %bitcast.3) | data formatting | bytes 262144
Async XLA Ops:
  0.6 1.2 %copy-start = (f32[1728,128]{1,0:T(8,128)S(1)}, f32[1728,128]{1,0:T(8,128)}, u32[]{:S(2)}) copy-start(f32[1728,128]{1,0:T(8,128)} %master_hbm.1) | copy-start | bytes 2654212
  1.8 0.9 %copy-start.1 = (bf16[1,4,16,8,128]{4,3,2,1,0:T(8,128)(2,1)S(1)}, bf16[1,4,16,8,128]{4,3,2,1,0:T(8,128)(2,1)}, u32[]{:S(2)}) copy-start(bf16[1,4,16,8,128]{4,3,2,1,0:T(8,128)(2,1)} %param.5) | copy-start | bytes 393220
  2.7 0.9 %copy-start.2 = (bf16[1,4,16,8,128]{4,3,2,1,0:T(8,128)(2,1)S(1)}, bf16[1,4,16,8,128]{4,3,2,1,0:T(8,128)(2,1)}, u32[]{:S(2)}) copy-start(bf16[1,4,16,8,128]{4,3,2,1,0:T(8,128)(2,1)} %param.6) | copy-start | bytes 393220
  3.6 53.1 %copy-start.3 = (f32[1728,128]{1,0:T(8,128)S(1)}, f32[1728,128]{1,0:T(8,128)}, u32[]{:S(2)}) copy-start(f32[1728,128]{1,0:T(8,128)} %param.8) | copy-start | bytes 2654212
  3.6 53.1 %copy-start.4 = (f32[1728,128]{1,0:T(8,128)S(1)}, f32[1728,128]{1,0:T(8,128)}, u32[]{:S(2)}) copy-start(f32[1728,128]{1,0:T(8,128)} %param.9) | copy-start | bytes 2654212

commit v3 on v2

--- a/solution.py
+++ b/solution.py
@@ -16,7 +16,7 @@
 C = 128
 HX, HY, CY = 3, 4, 2
 MESH = pl.DeviceIdType.MESH
-VMEM = pltpu.VMEM
+VMEM, HBM = pltpu.VMEM, pltpu.HBM
 f32, bf16 = jnp.float32, jnp.bfloat16
 
 
@@ -46,12 +46,24 @@
     Q = H // 4
     N = 3
     part_rows = Q // N
-    load = pltpu.make_async_copy(master_hbm, master, msem)
+    inner = (pl.ds(HX, sx), pl.ds(8 * HY, ry)), (pl.ds(1, sx), pl.ds(8 * CY, ry))
+    load = pltpu.make_async_copy(master_hbm, master, msem.at[0])
+    fields = [
+        pltpu.make_async_copy(vol, vext.at[inner[0]], msem.at[1]),
+        pltpu.make_async_copy(cot, cext.at[inner[1]], msem.at[2]),
+    ]
     load.start()
+    for copy in fields:
+        copy.start()
     here = {"x": (d, flip(x, bx, 1), y), "y": (d, x, flip(y, by, 2)), "c": (d, x, flip(y, bc, 1))}
 
-    vext[...] = jnp.zeros_like(vext)
-    cext[...] = jnp.zeros_like(cext)
+    for ref, hx, hy in ((vext, HX, 8 * HY), (cext, 1, 8 * CY)):
+        end = jnp.zeros((hx, *ref.shape[1:]), bf16)
+        side = jnp.zeros((sx, hy, C), bf16)
+        ref[:hx] = end
+        ref[hx + sx :] = end
+        ref[hx : hx + sx, :hy] = side
+        ref[hx : hx + sx, hy + ry :] = side
     around = [(i, j) for i in (-1, 0, 1) for j in (-1, 0, 1) if (i, j) != (0, 0)]
 
     def exists(i, j):
@@ -78,8 +90,6 @@
         pl.semaphore_signal(barrier, inc=1, device_id=(lax.rem(d + t, D), x, y), device_id_type=MESH)
     total = total + (D - 1)
 
-    vext[pl.ds(HX, sx), pl.ds(8 * HY, ry)] = vol[...]
-    cext[pl.ds(1, sx), pl.ds(8 * CY, ry)] = cot[...]
     load.wait()
     w[pl.ds(pl.multiple_of(d * H, 16), H)] = master[...].astype(bf16)
     pl.semaphore_wait(barrier, total)
@@ -185,15 +195,17 @@
             for copy in halo(7 - n, -i, -j):
                 copy.wait_recv()
 
+    for copy in fields:
+        copy.wait()
     yield
 
     steps = [(t, n) for t in range(1, D) for n in range(N)]
     behind = 0
     for at in range(N, len(steps)):
         relay(*steps[at])
-        if at >= N:
-            pass_on(*steps[behind])
-            behind += 1
+        pass_on(*steps[behind])
+        behind += 1
+        yield
     for at in range(behind, len(steps)):
         pass_on(*steps[at])
 
@@ -264,11 +276,14 @@
     d1[...] = jnp.zeros_like(d1)
     d2[...] = jnp.zeros_like(d2)
 
-    @pl.loop(0, sx + 6)
-    def _(s):
-        unfold(vext[s].astype(f32), 8, n1, x1.at[s])
-
-    yield
+    cuts = 3 * (D - 2)
+    edges = [(sx + 6) * k // cuts for k in range(cuts + 1)]
+    for low, high in zip(edges, edges[1:]):
+        @pl.loop(low, high)
+        def _(s):
+            unfold(vext[s].astype(f32), 8, n1, x1.at[s])
+
+        yield
 
     def conv(source, kernel, at, size, contract):
         total = None
@@ -513,7 +528,9 @@
     compute = compute_phases(counts, vext, cext, w, act, g, *fields)
     reduce = reduce_phases(counts, g, out, *sums)
     next(gather)
-    next(compute)
+    for _ in range(3 * (counts[0] - 2)):
+        next(compute)
+        next(gather)
     next(gather)
     next(compute)
     next(gather)
@@ -526,11 +543,36 @@
     next(gather)
 
 
-def adam_update(master, moment_one, moment_two, gradient):
-    new_one = beta_one * moment_one + (1.0 - beta_one) * gradient
-    new_two = beta_two * moment_two + (1.0 - beta_two) * gradient * gradient
-    update = new_one / (1.0 - beta_one**10) / (jnp.sqrt(new_two / (1.0 - beta_two**10)) + epsilon)
-    return (master - learn_rate * update, new_one, new_two)
+def finish_kernel(act_in, rows, master, one, two, act, new_master, new_one, new_two, o0, o1, o2, i0, i1, i2, sem, fsem):
+    H = master.shape[0]
+    parts = 4
+    n = H // parts
+    loads = []
+    for i in range(parts):
+        at = pl.ds(i * n, n)
+        for k, (src, dst) in enumerate(((master, i0), (one, i1), (two, i2))):
+            copy = pltpu.make_async_copy(src.at[at], dst.at[at], fsem.at[3 * i + k])
+            copy.start()
+            loads.append(copy)
+    copies = [pltpu.make_async_copy(act_in, act, sem.at[0])]
+    copies[0].start()
+    for i in range(parts):
+        at = pl.ds(i * n, n)
+        gradient = rows[at].astype(f32)
+        for copy in loads[3 * i : 3 * i + 3]:
+            copy.wait()
+        first = beta_one * i1[at] + (1.0 - beta_one) * gradient
+        second = beta_two * i2[at] + (1.0 - beta_two) * gradient * gradient
+        step = first / (1.0 - beta_one**10) / (jnp.sqrt(second / (1.0 - beta_two**10)) + epsilon)
+        o1[at] = first
+        o2[at] = second
+        o0[at] = i0[at] - learn_rate * step
+        for k, (src, dst) in enumerate(((o0, new_master), (o1, new_one), (o2, new_two))):
+            copy = pltpu.make_async_copy(src.at[at], dst.at[at], sem.at[1 + 3 * i + k])
+            copy.start()
+            copies.append(copy)
+    for copy in copies:
+        copy.wait()
 
 
 def per_device(counts, volume, cotangent, master, moment_one, moment_two):
@@ -550,7 +592,7 @@
             jax.ShapeDtypeStruct((sx, ry, width), bf16),
             jax.ShapeDtypeStruct((H, width), bf16),
         ),
-        in_specs=[whole, whole, pl.BlockSpec(memory_space=pl.ANY)],
+        in_specs=[pl.BlockSpec(memory_space=HBM)] * 3,
         out_specs=(whole,) * 2,
         scratch_shapes=[
             VMEM((H, width), f32),
@@ -558,7 +600,7 @@
             VMEM((sx + 2, ry + 16 * CY, width), bf16),
             VMEM((D * H, width), bf16),
             VMEM((D * H, width), bf16),
-            sem(()), sem((2, 8)), sem((2, 8)), sem((5, D, 3)), sem((5, D, 3)),
+            sem((3,)), sem((2, 8)), sem((2, 8)), sem((5, D, 3)), sem((5, D, 3)),
             VMEM((sx + 6, n1, 9 * C), bf16),
             VMEM((sx + 4, n2, 9 * C), bf16),
             VMEM((sx + 2, ry, 9 * C), bf16),
@@ -578,12 +620,21 @@
             sem((D - 1,)), sem((D - 1,)), sem((3,)), sem((3,)), sem((2,)), sem((2,)),
         ],
         compiler_params=pltpu.CompilerParams(
-            collective_id=0, has_side_effects=True, vmem_limit_bytes=44 * 2**20
+            collective_id=0, has_side_effects=True, vmem_limit_bytes=63 * 2**20
         ),
         cost_estimate=pl.CostEstimate(flops=4 * 10**10, bytes_accessed=10**8, transcendentals=10**6),
         name="step",
     )(vol, cot, master)
-    new_master, new_one, new_two = adam_update(master, moment_one, moment_two, rows.astype(f32))
+    table = jax.ShapeDtypeStruct((H, width), f32)
+    act, new_master, new_one, new_two = pl.pallas_call(
+        finish_kernel,
+        out_shape=(jax.ShapeDtypeStruct((sx, ry, width), bf16), table, table, table),
+        in_specs=[pl.BlockSpec(memory_space=pl.ANY), whole] + [pl.BlockSpec(memory_space=pl.ANY)] * 3,
+        out_specs=(pl.BlockSpec(memory_space=HBM),) * 4,
+        scratch_shapes=[VMEM((H, width), f32)] * 6 + [sem((13,)), sem((12,))],
+        compiler_params=pltpu.CompilerParams(vmem_limit_bytes=63 * 2**20),
+        name="finish",
+    )(act, rows, master, moment_one, moment_two)
     return (act.reshape(volume.shape), new_master, new_one, new_two)
 
 

time: 59.4 us -> 61.1 us (1.029)
  Pallas kernels: 53.1 us -> 60.2 us
  local copies, waits for them, and re-layouts: 3.63 us -> 0 us
  other arithmetic: 1.87 us -> 0 us
    pallas_call x0 -> x1, Pallas kernels: none -> 6.33 us  [per_device(): pl.pallas_call(finish_kernel, out_shape=(jax.ShapeDtypeStruct((sx, ry, wi...]
    unnamed x11 -> x0, local copies, waits for them, and re-layouts: 3.63 us -> none
    sub x1 -> x0, other arithmetic: 1.87 us -> none  [adam_update(): return (master - learn_rate * update, new_one, new_two)]
    pallas_call x1, Pallas kernels: 53.1 us -> 53.9 us  [per_device(): pl.pallas_call(functools.partial(step_kernel, counts), out_shape=(jax.Sha...]
where the time goes in v3:
time: 61.1 us; the launch traced here: 60.9 us
  Pallas kernels  60.2 us (99%)
  between operations  0.64 us (1%)
    pallas_call x1, Pallas kernels, per_device(): pl.pallas_call(functools.partial(step_kernel, counts), out_shape=(jax.Sha...  53.9 us
    pallas_call x1, Pallas kernels, per_device(): pl.pallas_call(finish_kernel, out_shape=(jax.ShapeDtypeStruct((sx, ry, wi...  6.33 us

profile of v3, /device:TPU:1, one launch (start us, length us, event | category | flops | bytes accessed | tf_op | source)
XLA Modules:
  0.0 60.9 jit_solution(10043564213661356309)
XLA Ops:
  0.6 53.9 %step.1 = (bf16[4,128,128]{2,1,0:T(8,128)(2,1)}, bf16[1728,128]{1,0:T(8,128)(2,1)}) custom-call(bf16[4,128,128]{2,1,0:T(8,128)(2,1)} %bitcast.3, bf16[4,128,128]{2,1,0:T(8,128)(2,1)} %bitcast.4, f32[1728,128]{1,0:T(8,128)} %master.1), custom_call_target="tpu_custom_call" | custom-call | flops 40000000000 | bytes 100000000 | tf_op jit(solution)/shard_map/step/pallas_call | solution.py:589
  54.5 6.3 %finish.1 = (bf16[4,128,128]{2,1,0:T(8,128)(2,1)}, f32[1728,128]{1,0:T(8,128)}, f32[1728,128]{1,0:T(8,128)}, f32[1728,128]{1,0:T(8,128)}) custom-call(bf16[4,128,128]{2,1,0:T(8,128)(2,1)} %get-tuple-element.10.act_in, bf16[1728,128]{1,0:T(8,128)(2,1)} %get-tuple-element.11.rows, f32[1728,128]{1,0:T(8,128)} %master.1, f32[1728,128]{1,0:T(8,128)} %one.1, ...), custom_call_target="tpu_custom_call" | custom-call | tf_op jit(solution)/shard_map/finish/pallas_call | solution.py:629

commit v4 on v3

--- a/solution.py
+++ b/solution.py
@@ -374,91 +374,107 @@
     d, x, y, bx, by, bc = place()
     H = out.shape[0]
     Q = H // 4
-    cut = Q // 32 * 16
     px, py, pc = (d, flip(x, bx, 1), y), (d, x, flip(y, by, 2)), (d, x, flip(y, bc, 1))
     pxy = (d, flip(x, bx, 1), flip(y, by, 2))
+    cut = (Q // 16 + 1) // 2 * 16
+    chunks = ((0, cut), (cut, Q - cut))
 
     def copy(src, dst, send, recv, target):
         return pltpu.make_async_remote_copy(
             src_ref=src, dst_ref=dst, send_sem=send, recv_sem=recv, device_id=target, device_id_type=MESH
         )
 
-    def quarter(s, q):
-        return pl.ds(pl.multiple_of(s * H + q * Q, 16), Q)
-
-    def stage1(s, b):
-        return copy(g.at[quarter(s, 2 * b + 1 - bc)], r1.at[s, b], s1.at[s, b], q1.at[s, b], pc)
+    def in_quarter(s, q, lo, n):
+        return pl.ds(pl.multiple_of(s * H + q * Q + lo, 16), n)
+
+    def stage1(s, b, h):
+        lo, n = chunks[h]
+        src = g.at[in_quarter(s, 2 * b + 1 - bc, lo, n)]
+        return copy(src, r1.at[s, b, pl.ds(lo, n)], s1.at[s, b, h], q1.at[s, b, h], pc)
 
     def bits(s):
         return (bx, by, px, py) if s % 2 == 0 else (by, bx, py, px)
 
-    def stage2(s):
+    def stage2(s, h):
         b, _, target, _ = bits(s)
-        return copy(a1.at[s, 1 - b], r2.at[s], s2.at[s], q2.at[s], target)
-
-    def halves(bit, body):
+        at = pl.ds(*chunks[h])
+        return copy(a1.at[s, 1 - b, at], r2.at[s, at], s2.at[s, h], q2.at[s, h], target)
+
+    def halves(bit, h, body):
+        lo, n = chunks[h]
+        m = n // 32 * 16
+
         @pl.when(bit == 0)
         def _():
-            body(0, cut, cut, Q - cut)
+            body(lo, m, lo + m, n - m)
 
         @pl.when(bit == 1)
         def _():
-            body(cut, Q - cut, 0, cut)
-
-    def stage3(s, lo, n):
-        target = bits(s)[3]
-        return copy(a2.at[s, pl.ds(lo, n)], r3.at[s, pl.ds(lo, n)], s3.at[s], q3.at[s], target)
-
-    def begin(s):
+            body(lo + m, n - m, lo, m)
+
+    def stage3(s, h, lo, n):
+        at = pl.ds(lo, n)
+        return copy(a2.at[s, at], r3.at[s, at], s3.at[s, h], q3.at[s, h], bits(s)[3])
+
+    def stage4(s, t, h, lo, n):
+        at = pl.ds(lo, n)
+        return copy(a3.at[s, at], r4.at[t - 1, at], s4.at[t - 1, h], q4.at[t - 1, h], (s, x, y))
+
+    def stage6(b, c, h):
+        lo, n = chunks[h]
+        ref = fin.at[pl.ds(pl.multiple_of((2 * b + c) * Q + lo, 16), n)]
+        return copy(ref, ref, s6.at[b, h], q6.at[b, h], pc)
+
+    def begin(s, h):
         for b in range(2):
-            stage1(s, b).start()
-
-    def after1(s):
+            stage1(s, b, h).start()
+
+    def after1(s, h):
+        lo, n = chunks[h]
+        at = pl.ds(lo, n)
         for b in range(2):
-            stage1(s, b).wait_recv()
-            a1[s, b] = (g[quarter(s, 2 * b + bc)].astype(f32) + r1[s, b].astype(f32)).astype(bf16)
-        stage2(s).start()
-
-    def after2(s):
-        stage2(s).wait_recv()
+            stage1(s, b, h).wait_recv()
+            mine = g[in_quarter(s, 2 * b + bc, lo, n)].astype(f32)
+            a1[s, b, at] = (mine + r1[s, b, at].astype(f32)).astype(bf16)
+        stage2(s, h).start()
+
+    def after2(s, h):
+        at = pl.ds(*chunks[h])
+        stage2(s, h).wait_recv()
         b = bits(s)[0]
-        a2[s] = (a1[s, b].astype(f32) + r2[s].astype(f32)).astype(bf16)
-        halves(bits(s)[1], lambda lo, n, olo, on: stage3(s, olo, on).start())
-
-    def stage4(s, t, lo, n):
-        return copy(a3.at[s, pl.ds(lo, n)], r4.at[t - 1, pl.ds(lo, n)], s4.at[t - 1], q4.at[t - 1], (s, x, y))
-
-    def after3(s):
+        a2[s, at] = (a1[s, b, at].astype(f32) + r2[s, at].astype(f32)).astype(bf16)
+        halves(bits(s)[1], h, lambda lo, n, olo, on: stage3(s, h, olo, on).start())
+
+    def after3(s, h):
         def add(lo, n, olo, on):
-            stage3(s, lo, n).wait_recv()
+            stage3(s, h, lo, n).wait_recv()
             at = pl.ds(lo, n)
             a3[s, at] = (a2[s, at].astype(f32) + r3[s, at].astype(f32)).astype(bf16)
             for t in range(1, D):
                 @pl.when(lax.rem(d + t, D) == s)
                 def _(t=t):
-                    stage4(s, t, lo, n).start()
-
-        halves(bits(s)[1], add)
+                    stage4(s, t, h, lo, n).start()
+
+        halves(bits(s)[1], h, add)
 
     early, late = range(D // 2, D), range(D // 2)
-    for s in early:
-        begin(s)
-    yield
-    for s in early:
-        after1(s)
-    yield
-    for s in late:
-        begin(s)
-    for s in early:
-        after2(s)
-    for s in late:
-        after1(s)
-    for s in early:
-        after3(s)
-    for s in late:
-        after2(s)
-    for s in late:
-        after3(s)
+
+    def each(group, *steps):
+        for fn, h in steps:
+            for s in group:
+                fn(s, h)
+
+    each(early, (begin, 0), (begin, 1))
+    yield
+    each(early, (after1, 0), (after1, 1))
+    yield
+    each(late, (begin, 0), (begin, 1))
+    each(early, (after2, 0), (after2, 1))
+    each(late, (after1, 0))
+    each(early, (after3, 0))
+    each(late, (after1, 1))
+    each(early, (after3, 1))
+    each(late, (after2, 0), (after3, 0), (after2, 1), (after3, 1))
 
     for s in range(D):
         @pl.when(d == s)
@@ -468,66 +484,78 @@
             def piece(fb, lo, n):
                 return fin.at[pl.ds(pl.multiple_of((2 * fb + bc) * Q + lo, 16), n)]
 
-            def share(k, fb, lo, n, target):
-                return copy(piece(fb, lo, n), piece(fb, lo, n), s5.at[k], q5.at[k], target)
+            def share(k, h, fb, lo, n, target):
+                return copy(piece(fb, lo, n), piece(fb, lo, n), s5.at[k, h], q5.at[k, h], target)
 
             targets = (partner, across, pxy)
 
-            def finish(lo, n, olo, on):
+            def total(h, lo, n):
                 at = pl.ds(lo, n)
-                total = a3[s, at].astype(f32)
+                value = a3[s, at].astype(f32)
                 for t in range(1, D):
-                    stage4(s, t, lo, n).wait_recv()
-                    total = total + r4[t - 1, at].astype(f32)
-                piece(b, lo, n)[...] = total.astype(bf16)
+                    stage4(s, t, h, lo, n).wait_recv()
+                    value = value + r4[t - 1, at].astype(f32)
+                piece(b, lo, n)[...] = value.astype(bf16)
                 for k in range(3):
-                    share(k, b, lo, n, targets[k]).start()
-                share(0, 1 - b, lo, n, partner).wait_recv()
-                share(1, b, olo, on, across).wait_recv()
-                share(2, 1 - b, olo, on, pxy).wait_recv()
-
-            halves(e, finish)
-
-    def stage6(b, c):
-        ref = fin.at[pl.ds(pl.multiple_of((2 * b + c) * Q, 16), Q)]
-        return copy(ref, ref, s6.at[b], q6.at[b], pc)
-
-    for b in range(2):
-        stage6(b, bc).start()
-    for b in range(2):
-        stage6(b, 1 - bc).wait_recv()
+                    share(k, h, b, lo, n, targets[k]).start()
+
+            def collect(h, lo, n, olo, on):
+                share(0, h, 1 - b, lo, n, partner).wait_recv()
+                share(1, h, b, olo, on, across).wait_recv()
+                share(2, h, 1 - b, olo, on, pxy).wait_recv()
+
+            for h in range(2):
+                halves(e, h, lambda lo, n, olo, on, h=h: total(h, lo, n))
+            for h in range(2):
+                halves(e, h, lambda lo, n, olo, on, h=h: collect(h, lo, n, olo, on))
+                for fb in range(2):
+                    stage6(fb, bc, h).start()
+
+    for h in range(2):
+        for b in range(2):
+            stage6(b, 1 - bc, h).wait_recv()
     out[...] = fin[...]
 
     for s in range(D):
+        for h in range(2):
+            for b in range(2):
+                stage1(s, b, h).wait_send()
+            stage2(s, h).wait_send()
+
+            def drain(lo, n, olo, on, s=s, h=h):
+                stage3(s, h, olo, on).wait_send()
+                for t in range(1, D):
+                    @pl.when(lax.rem(d + t, D) == s)
+                    def _(t=t):
+                        stage4(s, t, h, lo, n).wait_send()
+
+                @pl.when(d == s)
+                def _():
+                    for k in range(3):
+                        ref = fin.at[pl.ds(lo, n)]
+                        copy(ref, ref, s5.at[k, h], q5.at[k, h], pc).wait_send()
+
+            halves(bits(s)[1], h, drain)
+    for h in range(2):
         for b in range(2):
-            stage1(s, b).wait_send()
-        stage2(s).wait_send()
-
-        def drain(lo, n, olo, on, s=s):
-            stage3(s, olo, on).wait_send()
-            for t in range(1, D):
-                @pl.when(lax.rem(d + t, D) == s)
-                def _(t=t):
-                    stage4(s, t, lo, n).wait_send()
-
-            @pl.when(d == s)
-            def _():
-                for k in range(3):
-                    ref = fin.at[pl.ds(lo, n)]
-                    copy(ref, ref, s5.at[k], q5.at[k], pc).wait_send()
-
-        halves(bits(s)[1], drain)
-    for b in range(2):
-        stage6(b, bc).wait_send()
-    yield
-
-
-def step_kernel(counts, vol, cot, master_hbm, act, out, master, vext, cext, w, g, *scratch):
+            stage6(b, bc, h).wait_send()
+    yield
+
+
+def step_kernel(
+    counts, vol, cot, master_hbm, one_hbm, two_hbm, act, out, master, one, two, vext, cext, w, g, *scratch
+):
     msem, moves, fields, sums = scratch[0], scratch[1:5], scratch[5:12], scratch[12:]
     gather = gather_phases(counts, vol, cot, master_hbm, master, vext, cext, w, msem, *moves)
     compute = compute_phases(counts, vext, cext, w, act, g, *fields)
     reduce = reduce_phases(counts, g, out, *sums)
     next(gather)
+    held = [
+        pltpu.make_async_copy(one_hbm, one, msem.at[3]),
+        pltpu.make_async_copy(two_hbm, two, msem.at[4]),
+    ]
+    for copy in held:
+        copy.start()
     for _ in range(3 * (counts[0] - 2)):
         next(compute)
         next(gather)
@@ -541,33 +569,26 @@
     next(compute)
     next(reduce)
     next(gather)
-
-
-def finish_kernel(act_in, rows, master, one, two, act, new_master, new_one, new_two, o0, o1, o2, i0, i1, i2, sem, fsem):
+    for copy in held:
+        copy.wait()
+
+
+def finish_kernel(act_in, rows, master, one, two, act, new_master, new_one, new_two, o0, o1, o2, sem):
     H = master.shape[0]
     parts = 4
     n = H // parts
-    loads = []
-    for i in range(parts):
-        at = pl.ds(i * n, n)
-        for k, (src, dst) in enumerate(((master, i0), (one, i1), (two, i2))):
-            copy = pltpu.make_async_copy(src.at[at], dst.at[at], fsem.at[3 * i + k])
-            copy.start()
-            loads.append(copy)
     copies = [pltpu.make_async_copy(act_in, act, sem.at[0])]
     copies[0].start()
     for i in range(parts):
         at = pl.ds(i * n, n)
         gradient = rows[at].astype(f32)
-        for copy in loads[3 * i : 3 * i + 3]:
-            copy.wait()
-        first = beta_one * i1[at] + (1.0 - beta_one) * gradient
-        second = beta_two * i2[at] + (1.0 - beta_two) * gradient * gradient
-        step = first / (1.0 - beta_one**10) / (jnp.sqrt(second / (1.0 - beta_two**10)) + epsilon)
+        first = beta_one * one[at] + (1.0 - beta_one) * gradient
+        second = beta_two * two[at] + (1.0 - beta_two) * gradient * gradient
         o1[at] = first
         o2[at] = second
-        o0[at] = i0[at] - learn_rate * step
-        for k, (src, dst) in enumerate(((o0, new_master), (o1, new_one), (o2, new_two))):
+        step = first / (1.0 - beta_one**10) / (jnp.sqrt(second / (1.0 - beta_two**10)) + epsilon)
+        o0[at] = master[at] - learn_rate * step
+        for k, (src, dst) in enumerate(((o1, new_one), (o2, new_two), (o0, new_master))):
             copy = pltpu.make_async_copy(src.at[at], dst.at[at], sem.at[1 + 3 * i + k])
             copy.start()
             copies.append(copy)
@@ -586,21 +607,24 @@
     vol = volume.reshape(sx, ry, width)
     cot = cotangent.reshape(sx, ry, width)
     n1, n2 = ry + 32, ry + 16
-    act, rows = pl.pallas_call(
+    table = jax.ShapeDtypeStruct((H, width), f32)
+    act, rows, *held = pl.pallas_call(
         functools.partial(step_kernel, counts),
         out_shape=(
             jax.ShapeDtypeStruct((sx, ry, width), bf16),
             jax.ShapeDtypeStruct((H, width), bf16),
+            table,
+            table,
+            table,
         ),
-        in_specs=[pl.BlockSpec(memory_space=HBM)] * 3,
-        out_specs=(whole,) * 2,
+        in_specs=[pl.BlockSpec(memory_space=HBM)] * 5,
+        out_specs=(whole,) * 5,
         scratch_shapes=[
-            VMEM((H, width), f32),
             VMEM((sx + 2 * HX, ry + 16 * HY, width), bf16),
             VMEM((sx + 2, ry + 16 * CY, width), bf16),
             VMEM((D * H, width), bf16),
             VMEM((D * H, width), bf16),
-            sem((3,)), sem((2, 8)), sem((2, 8)), sem((5, D, 3)), sem((5, D, 3)),
+            sem((5,)), sem((2, 8)), sem((2, 8)), sem((5, D, 3)), sem((5, D, 3)),
             VMEM((sx + 6, n1, 9 * C), bf16),
             VMEM((sx + 4, n2, 9 * C), bf16),
             VMEM((sx + 2, ry, 9 * C), bf16),
@@ -616,25 +640,24 @@
             VMEM((D, Q, width), bf16),
             VMEM((D - 1, Q, width), bf16),
             VMEM((H, width), bf16),
-            sem((D, 2)), sem((D, 2)), sem((D,)), sem((D,)), sem((D,)), sem((D,)),
-            sem((D - 1,)), sem((D - 1,)), sem((3,)), sem((3,)), sem((2,)), sem((2,)),
+            sem((D, 2, 2)), sem((D, 2, 2)), sem((D, 2)), sem((D, 2)), sem((D, 2)), sem((D, 2)),
+            sem((D - 1, 2)), sem((D - 1, 2)), sem((3, 2)), sem((3, 2)), sem((2, 2)), sem((2, 2)),
         ],
         compiler_params=pltpu.CompilerParams(
-            collective_id=0, has_side_effects=True, vmem_limit_bytes=63 * 2**20
+            collective_id=0, has_side_effects=True, vmem_limit_bytes=50 * 2**20
         ),
         cost_estimate=pl.CostEstimate(flops=4 * 10**10, bytes_accessed=10**8, transcendentals=10**6),
         name="step",
-    )(vol, cot, master)
-    table = jax.ShapeDtypeStruct((H, width), f32)
+    )(vol, cot, master, moment_one, moment_two)
     act, new_master, new_one, new_two = pl.pallas_call(
         finish_kernel,
         out_shape=(jax.ShapeDtypeStruct((sx, ry, width), bf16), table, table, table),
-        in_specs=[pl.BlockSpec(memory_space=pl.ANY), whole] + [pl.BlockSpec(memory_space=pl.ANY)] * 3,
+        in_specs=[whole] * 5,
         out_specs=(pl.BlockSpec(memory_space=HBM),) * 4,
-        scratch_shapes=[VMEM((H, width), f32)] * 6 + [sem((13,)), sem((12,))],
-        compiler_params=pltpu.CompilerParams(vmem_limit_bytes=63 * 2**20),
+        scratch_shapes=[VMEM((H, width), f32)] * 3 + [sem((13,))],
+        compiler_params=pltpu.CompilerParams(vmem_limit_bytes=8 * 2**20),
         name="finish",
-    )(act, rows, master, moment_one, moment_two)
+    )(act, rows, *held)
     return (act.reshape(volume.shape), new_master, new_one, new_two)
 
 

time: 61.1 us -> 59.4 us (0.972)
  Pallas kernels: 60.2 us -> 56.8 us
  local copies, waits for them, and re-layouts: 0 us -> 1.8 us
    pallas_call x1, Pallas kernels: 6.33 us -> 1.67 us  [per_device(): pl.pallas_call(finish_kernel, out_shape=(jax.ShapeDtypeStruct((sx, ry, wi...]
    unnamed x0 -> x4, local copies, waits for them, and re-layouts: none -> 1.8 us
    pallas_call x1, Pallas kernels: 53.9 us -> 55.1 us  [per_device(): pl.pallas_call(functools.partial(step_kernel, counts), out_shape=(jax.Sha...]
where the time goes in v4:
time: 59.4 us; the launch traced here: 59.2 us
  Pallas kernels  56.8 us (96%)
  local copies, waits for them, and re-layouts  1.8 us (3%)
  between operations  0.65 us (1%)
    pallas_call x1, Pallas kernels, per_device(): pl.pallas_call(functools.partial(step_kernel, counts), out_shape=(jax.Sha...  55.1 us
    unnamed x4, local copies, waits for them, and re-layouts  1.8 us
    pallas_call x1, Pallas kernels, per_device(): pl.pallas_call(finish_kernel, out_shape=(jax.ShapeDtypeStruct((sx, ry, wi...  1.67 us

profile of v4, /device:TPU:1, one launch (start us, length us, event | category | flops | bytes accessed | tf_op | source)
XLA Modules:
  0.0 59.2 jit_solution(12273205223488271721)
XLA Ops:
  0.6 0.0 copy-start
  0.6 0.9 %copy-done = bf16[1,4,16,8,128]{4,3,2,1,0:T(8,128)(2,1)S(1)} copy-done((bf16[1,4,16,8,128]{4,3,2,1,0:T(8,128)(2,1)S(1)}, bf16[1,4,16,8,128]{4,3,2,1,0:T(8,128)(2,1)}, u32[]{:S(2)}) %copy-start) | copy-done | bytes 131096
  1.5 0.0 copy-start.1
  1.5 0.9 %copy-done.1 = bf16[1,4,16,8,128]{4,3,2,1,0:T(8,128)(2,1)S(1)} copy-done((bf16[1,4,16,8,128]{4,3,2,1,0:T(8,128)(2,1)S(1)}, bf16[1,4,16,8,128]{4,3,2,1,0:T(8,128)(2,1)}, u32[]{:S(2)}) %copy-start.1) | copy-done | bytes 131096
  2.4 55.1 %step.1 = (bf16[4,128,128]{2,1,0:T(8,128)(2,1)S(1)}, bf16[1728,128]{1,0:T(8,128)(2,1)S(1)}, f32[1728,128]{1,0:T(8,128)S(1)}, f32[1728,128]{1,0:T(8,128)S(1)}, f32[1728,128]{1,0:T(8,128)S(1)}) custom-call(bf16[4,128,128]{2,1,0:T(8,128)(2,1)S(1)} %bitcast.3, bf16[4,128,128]{2,1,0:T(8,128)(2,1)S(1)} %bitcast.4, f32[1728,128]{1,0:T(8,128)} %master_hbm.1, ...), custom_call_target="tpu_custom_call" | custom-call | flops 40000000000 | bytes 100000000 | tf_op jit(solution)/shard_map/step/pallas_call | solution.py:611
  57.6 1.7 %finish.1 = (bf16[4,128,128]{2,1,0:T(8,128)(2,1)}, f32[1728,128]{1,0:T(8,128)}, f32[1728,128]{1,0:T(8,128)}, f32[1728,128]{1,0:T(8,128)}) custom-call(bf16[4,128,128]{2,1,0:T(8,128)(2,1)S(1)} %get-tuple-element.13.act_in, bf16[1728,128]{1,0:T(8,128)(2,1)S(1)} %get-tuple-element.14.rows, f32[1728,128]{1,0:T(8,128)S(1)} %get-tuple-element.15.master, ...), custom_call_target="tpu_custom_call" | custom-call | tf_op jit(solution)/shard_map/finish/pallas_call | solution.py:652
Async XLA Ops:
  0.6 0.9 %copy-start = (bf16[1,4,16,8,128]{4,3,2,1,0:T(8,128)(2,1)S(1)}, bf16[1,4,16,8,128]{4,3,2,1,0:T(8,128)(2,1)}, u32[]{:S(2)}) copy-start(bf16[1,4,16,8,128]{4,3,2,1,0:T(8,128)(2,1)} %param.5) | copy-start | bytes 393220
  1.5 0.9 %copy-start.1 = (bf16[1,4,16,8,128]{4,3,2,1,0:T(8,128)(2,1)S(1)}, bf16[1,4,16,8,128]{4,3,2,1,0:T(8,128)(2,1)}, u32[]{:S(2)}) copy-start(bf16[1,4,16,8,128]{4,3,2,1,0:T(8,128)(2,1)} %param.6) | copy-start | bytes 393220

commit v5 on v4

--- a/solution.py
+++ b/solution.py
@@ -199,17 +199,7 @@
         copy.wait()
     yield
 
-    steps = [(t, n) for t in range(1, D) for n in range(N)]
-    behind = 0
-    for at in range(N, len(steps)):
-        relay(*steps[at])
-        pass_on(*steps[behind])
-        behind += 1
-        yield
-    for at in range(behind, len(steps)):
-        pass_on(*steps[at])
-
-    for low, high in ((0, D // 2), (D // 2, D)):
+    def settle(low, high):
         for s in range(low, high):
             @pl.when(d != s)
             def _(s=s):
@@ -218,7 +208,18 @@
                     sibling(z, 2 * bit(z) + 1 - bc, 3, n).wait_recv()
                     sibling(z, 2 * (1 - bit(z)) + 1 - bc, 4, n).wait_recv()
 
+    for n in range(N):
+        relay(2, n)
+        pass_on(1, n)
         yield
+    yield settle
+    for t in range(3, D):
+        for n in range(N):
+            relay(t, n)
+            pass_on(t - 1, n)
+    for n in range(N):
+        pass_on(D - 1, n)
+    yield
 
     for s in range(D):
         z = jnp.int32(s)
@@ -265,7 +266,7 @@
             out[:, k * C : (k + 1) * C] = views[c][first + 8 * b : first + 8 * b + rows].astype(bf16)
 
 
-def compute_phases(counts, vext, cext, w, act, grad, x1, x2, x3, first, kt, d1, d2):
+def compute_phases(counts, vext, cext, w, act, grad, x1, x2, x3, first, kt, kk, d1, d2):
     D, GX, GY = counts
     sx = vext.shape[0] - 2 * HX
     ry = vext.shape[1] - 16 * HY
@@ -276,7 +277,7 @@
     d1[...] = jnp.zeros_like(d1)
     d2[...] = jnp.zeros_like(d2)
 
-    cuts = 3 * (D - 2)
+    cuts = 3
     edges = [(sx + 6) * k // cuts for k in range(cuts + 1)]
     for low, high in zip(edges, edges[1:]):
         @pl.loop(low, high)
@@ -285,35 +286,42 @@
 
         yield
 
-    def conv(source, kernel, at, size, contract):
-        total = None
-        for a in range(3):
-            lhs = source[pl.ds(at + a, size)]
-            lhs = lhs.reshape(size * lhs.shape[1], L)
-            term = lax.dot_general(
-                lhs, kernel(a), (((1,), (contract,)), ((), ())), preferred_element_type=f32
+    def conv(source, pair, last, at, size, contract):
+        def product(begin, slices, kernel):
+            lhs = source[pl.ds(begin, slices)].reshape(slices * source.shape[1], L)
+            return lax.dot_general(
+                lhs, kernel, (((1,), (contract,)), ((), ())), preferred_element_type=f32
             )
-            total = term if total is None else total + term
-        return total
+
+        n = source.shape[1]
+        both = product(at, size + 1, pair)
+        return both[: size * n, :C] + both[n:, C:] + product(at + 2, size, last)
+
+    def load_pair(base):
+        for a in range(2):
+            kk[:, a * C : (a + 1) * C] = w[base + a * L : base + (a + 1) * L]
 
     half = (sx + 4) // 2
     row = lax.broadcasted_iota(jnp.int32, (n1, C), 0)
     y_at = lax.div(row, 8) - 2 + gy * (ry // 8)
     y_ok = jnp.where((y_at >= 0) & (y_at < GY * (ry // 8)), 1.0, 0.0)
 
-    @pl.loop(0, 2)
-    def _(p):
-        pre = conv(x1, lambda a: w[a * L : (a + 1) * L], p * half, half, 0)
-        for i in range(half):
-            piece = pre[i * n1 : (i + 1) * n1]
-            s = p * half + i
-            first[s] = piece
-            x_at = s - 2 + gx * sx
-            x_ok = jnp.where((x_at >= 0) & (x_at < GX * sx), 1.0, 0.0)
-            hidden = gelu_value(piece).astype(bf16).astype(f32) * (y_ok * x_ok)
-            unfold(hidden, 0, n2, x2.at[s])
-
-    yield
+    def first_layer():
+        load_pair(0)
+
+        @pl.loop(0, 2)
+        def _(p):
+            pre = conv(x1, kk[...], w[2 * L : 3 * L], p * half, half, 0)
+            for i in range(half):
+                piece = pre[i * n1 : (i + 1) * n1]
+                s = p * half + i
+                first[s] = piece
+                x_at = s - 2 + gx * sx
+                x_ok = jnp.where((x_at >= 0) & (x_at < GX * sx), 1.0, 0.0)
+                hidden = gelu_value(piece).astype(bf16).astype(f32) * (y_ok * x_ok)
+                unfold(hidden, 0, n2, x2.at[s])
+
+    yield first_layer
 
     for a in range(3):
         for k in range(9):
@@ -321,10 +329,11 @@
             kt[a, :, k * C : (k + 1) * C] = w[base : base + C]
 
     half2 = (sx + 2) // 2
+    load_pair(27 * C)
 
     @pl.loop(0, 2)
     def _(p):
-        pre = conv(x2, lambda a: w[27 * C + a * L : 27 * C + (a + 1) * L], p * half2, half2, 0)
+        pre = conv(x2, kk[...], w[27 * C + 2 * L : 27 * C + 3 * L], p * half2, half2, 0)
         for i in range(half2):
             piece = pre[i * n2 : (i + 1) * n2]
             s = p * half2 + i
@@ -356,7 +365,7 @@
     weight_grad(x2, 1, d2, 27 * C)
     yield
 
-    back = conv(x3, lambda a: kt[a], 0, sx, 1)
+    back = conv(x3, kt[0:2].reshape(2 * C, L), kt[2], 0, sx, 1)
     for i in range(sx):
         piece = back[i * ry : (i + 1) * ry]
         slope = gelu_slope(first[i + 2][16 : 16 + ry])
@@ -469,12 +478,20 @@
     each(early, (after1, 0), (after1, 1))
     yield
     each(late, (begin, 0), (begin, 1))
+    yield
     each(early, (after2, 0), (after2, 1))
     each(late, (after1, 0))
     each(early, (after3, 0))
     each(late, (after1, 1))
     each(early, (after3, 1))
     each(late, (after2, 0), (after3, 0), (after2, 1), (after3, 1))
+
+    for s in range(D):
+        for h in range(2):
+            for b in range(2):
+                stage1(s, b, h).wait_send()
+            stage2(s, h).wait_send()
+            halves(bits(s)[1], h, lambda lo, n, olo, on, s=s, h=h: stage3(s, h, olo, on).wait_send())
 
     for s in range(D):
         @pl.when(d == s)
@@ -511,19 +528,9 @@
                 for fb in range(2):
                     stage6(fb, bc, h).start()
 
-    for h in range(2):
-        for b in range(2):
-            stage6(b, 1 - bc, h).wait_recv()
-    out[...] = fin[...]
-
     for s in range(D):
         for h in range(2):
-            for b in range(2):
-                stage1(s, b, h).wait_send()
-            stage2(s, h).wait_send()
-
             def drain(lo, n, olo, on, s=s, h=h):
-                stage3(s, h, olo, on).wait_send()
                 for t in range(1, D):
                     @pl.when(lax.rem(d + t, D) == s)
                     def _(t=t):
@@ -536,6 +543,12 @@
                         copy(ref, ref, s5.at[k, h], q5.at[k, h], pc).wait_send()
 
             halves(bits(s)[1], h, drain)
+
+    for h in range(2):
+        for b in range(2):
+            stage6(b, 1 - bc, h).wait_recv()
+    out[...] = fin[...]
+
     for h in range(2):
         for b in range(2):
             stage6(b, bc, h).wait_send()
@@ -545,7 +558,7 @@
 def step_kernel(
     counts, vol, cot, master_hbm, one_hbm, two_hbm, act, out, master, one, two, vext, cext, w, g, *scratch
 ):
-    msem, moves, fields, sums = scratch[0], scratch[1:5], scratch[5:12], scratch[12:]
+    msem, moves, fields, sums = scratch[0], scratch[1:5], scratch[5:13], scratch[13:]
     gather = gather_phases(counts, vol, cot, master_hbm, master, vext, cext, w, msem, *moves)
     compute = compute_phases(counts, vext, cext, w, act, g, *fields)
     reduce = reduce_phases(counts, g, out, *sums)
@@ -556,12 +569,27 @@
     ]
     for copy in held:
         copy.start()
-    for _ in range(3 * (counts[0] - 2)):
+    for _ in range(3):
         next(compute)
         next(gather)
+    settle = next(gather)
+    first_layer = next(compute)
+    D = counts[0]
+    low = lax.axis_index("dp") < D // 2
+
+    @pl.when(low)
+    def _():
+        settle(0, D // 2)
+        first_layer()
+
     next(gather)
-    next(compute)
-    next(gather)
+
+    @pl.when(jnp.logical_not(low))
+    def _():
+        settle(0, D // 2)
+        first_layer()
+
+    settle(D // 2, D)
     next(compute)
     next(reduce)
     next(compute)
@@ -569,6 +597,7 @@
     next(compute)
     next(reduce)
     next(gather)
+    next(reduce)
     for copy in held:
         copy.wait()
 
@@ -630,6 +659,7 @@
             VMEM((sx + 2, ry, 9 * C), bf16),
             VMEM((sx + 4, n1, C), f32),
             VMEM((3, C, 9 * C), bf16),
+            VMEM((9 * C, 2 * C), bf16),
             VMEM((sx + 2, n1, 3 * C), bf16),
             VMEM((sx + 2, n2, 3 * C), bf16),
             VMEM((D, 2, Q, width), bf16),

time: 59.4 us -> 58.6 us (0.987)
  Pallas kernels: 56.8 us -> 55.9 us
    pallas_call x1, Pallas kernels: 55.1 us -> 54.3 us  [per_device(): pl.pallas_call(functools.partial(step_kernel, counts), out_shape=(jax.Sha...]
where the time goes in v5:
time: 58.6 us; the launch traced here: 58.4 us
  Pallas kernels  55.9 us (95%)
  local copies, waits for them, and re-layouts  1.8 us (3%)
  between operations  0.65 us (1%)
    pallas_call x1, Pallas kernels, per_device(): pl.pallas_call(functools.partial(step_kernel, counts), out_shape=(jax.Sha...  54.3 us
    unnamed x4, local copies, waits for them, and re-layouts  1.8 us
    pallas_call x1, Pallas kernels, per_device(): pl.pallas_call(finish_kernel, out_shape=(jax.ShapeDtypeStruct((sx, ry, wi...  1.67 us

profile of v5, /device:TPU:1, one launch (start us, length us, event | category | flops | bytes accessed | tf_op | source)
XLA Modules:
  0.0 58.4 jit_solution(7720730342558477123)
XLA Ops:
  0.6 0.0 copy-start
  0.6 0.9 %copy-done = bf16[1,4,16,8,128]{4,3,2,1,0:T(8,128)(2,1)S(1)} copy-done((bf16[1,4,16,8,128]{4,3,2,1,0:T(8,128)(2,1)S(1)}, bf16[1,4,16,8,128]{4,3,2,1,0:T(8,128)(2,1)}, u32[]{:S(2)}) %copy-start) | copy-done | bytes 131096
  1.5 0.0 copy-start.1
  1.5 0.9 %copy-done.1 = bf16[1,4,16,8,128]{4,3,2,1,0:T(8,128)(2,1)S(1)} copy-done((bf16[1,4,16,8,128]{4,3,2,1,0:T(8,128)(2,1)S(1)}, bf16[1,4,16,8,128]{4,3,2,1,0:T(8,128)(2,1)}, u32[]{:S(2)}) %copy-start.1) | copy-done | bytes 131096
  2.4 54.3 %step.1 = (bf16[4,128,128]{2,1,0:T(8,128)(2,1)S(1)}, bf16[1728,128]{1,0:T(8,128)(2,1)S(1)}, f32[1728,128]{1,0:T(8,128)S(1)}, f32[1728,128]{1,0:T(8,128)S(1)}, f32[1728,128]{1,0:T(8,128)S(1)}) custom-call(bf16[4,128,128]{2,1,0:T(8,128)(2,1)S(1)} %bitcast.3, bf16[4,128,128]{2,1,0:T(8,128)(2,1)S(1)} %bitcast.4, f32[1728,128]{1,0:T(8,128)} %master_hbm.1, ...), custom_call_target="tpu_custom_call" | custom-call | flops 40000000000 | bytes 100000000 | tf_op jit(solution)/shard_map/step/pallas_call | solution.py:640
  56.7 1.7 %finish.1 = (bf16[4,128,128]{2,1,0:T(8,128)(2,1)}, f32[1728,128]{1,0:T(8,128)}, f32[1728,128]{1,0:T(8,128)}, f32[1728,128]{1,0:T(8,128)}) custom-call(bf16[4,128,128]{2,1,0:T(8,128)(2,1)S(1)} %get-tuple-element.13.act_in, bf16[1728,128]{1,0:T(8,128)(2,1)S(1)} %get-tuple-element.14.rows, f32[1728,128]{1,0:T(8,128)S(1)} %get-tuple-element.15.master, ...), custom_call_target="tpu_custom_call" | custom-call | tf_op jit(solution)/shard_map/finish/pallas_call | solution.py:682
Async XLA Ops:
  0.6 0.9 %copy-start = (bf16[1,4,16,8,128]{4,3,2,1,0:T(8,128)(2,1)S(1)}, bf16[1,4,16,8,128]{4,3,2,1,0:T(8,128)(2,1)}, u32[]{:S(2)}) copy-start(bf16[1,4,16,8,128]{4,3,2,1,0:T(8,128)(2,1)} %param.5) | copy-start | bytes 393220
  1.5 0.9 %copy-start.1 = (bf16[1,4,16,8,128]{4,3,2,1,0:T(8,128)(2,1)S(1)}, bf16[1,4,16,8,128]{4,3,2,1,0:T(8,128)(2,1)}, u32[]{:S(2)}) copy-start(bf16[1,4,16,8,128]{4,3,2,1,0:T(8,128)(2,1)} %param.6) | copy-start | bytes 393220

commit v6 on v5

--- a/solution.py
+++ b/solution.py
@@ -44,7 +44,7 @@
     sx, ry = vol.shape[0], vol.shape[1]
     H = master.shape[0]
     Q = H // 4
-    N = 3
+    N = 1
     part_rows = Q // N
     inner = (pl.ds(HX, sx), pl.ds(8 * HY, ry)), (pl.ds(1, sx), pl.ds(8 * CY, ry))
     load = pltpu.make_async_copy(master_hbm, master, msem.at[0])
@@ -277,7 +277,7 @@
     d1[...] = jnp.zeros_like(d1)
     d2[...] = jnp.zeros_like(d2)
 
-    cuts = 3
+    cuts = 1
     edges = [(sx + 6) * k // cuts for k in range(cuts + 1)]
     for low, high in zip(edges, edges[1:]):
         @pl.loop(low, high)
@@ -385,8 +385,8 @@
     Q = H // 4
     px, py, pc = (d, flip(x, bx, 1), y), (d, x, flip(y, by, 2)), (d, x, flip(y, bc, 1))
     pxy = (d, flip(x, bx, 1), flip(y, by, 2))
-    cut = (Q // 16 + 1) // 2 * 16
-    chunks = ((0, cut), (cut, Q - cut))
+    chunks = ((0, Q),)
+    NH = len(chunks)
 
     def copy(src, dst, send, recv, target):
         return pltpu.make_async_remote_copy(
@@ -473,21 +473,19 @@
             for s in group:
                 fn(s, h)
 
-    each(early, (begin, 0), (begin, 1))
-    yield
-    each(early, (after1, 0), (after1, 1))
-    yield
-    each(late, (begin, 0), (begin, 1))
-    yield
-    each(early, (after2, 0), (after2, 1))
+    each(early, (begin, 0))
+    yield
+    each(early, (after1, 0))
+    yield
+    each(late, (begin, 0))
+    yield
+    each(early, (after2, 0))
     each(late, (after1, 0))
     each(early, (after3, 0))
-    each(late, (after1, 1))
-    each(early, (after3, 1))
-    each(late, (after2, 0), (after3, 0), (after2, 1), (after3, 1))
+    each(late, (after2, 0), (after3, 0))
 
     for s in range(D):
-        for h in range(2):
+        for h in range(NH):
             for b in range(2):
                 stage1(s, b, h).wait_send()
             stage2(s, h).wait_send()
@@ -521,15 +519,15 @@
                 share(1, h, b, olo, on, across).wait_recv()
                 share(2, h, 1 - b, olo, on, pxy).wait_recv()
 
-            for h in range(2):
+            for h in range(NH):
                 halves(e, h, lambda lo, n, olo, on, h=h: total(h, lo, n))
-            for h in range(2):
+            for h in range(NH):
                 halves(e, h, lambda lo, n, olo, on, h=h: collect(h, lo, n, olo, on))
                 for fb in range(2):
                     stage6(fb, bc, h).start()
 
     for s in range(D):
-        for h in range(2):
+        for h in range(NH):
             def drain(lo, n, olo, on, s=s, h=h):
                 for t in range(1, D):
                     @pl.when(lax.rem(d + t, D) == s)
@@ -544,12 +542,12 @@
 
             halves(bits(s)[1], h, drain)
 
-    for h in range(2):
+    for h in range(NH):
         for b in range(2):
             stage6(b, 1 - bc, h).wait_recv()
     out[...] = fin[...]
 
-    for h in range(2):
+    for h in range(NH):
         for b in range(2):
             stage6(b, bc, h).wait_send()
     yield
@@ -569,7 +567,7 @@
     ]
     for copy in held:
         copy.start()
-    for _ in range(3):
+    for _ in range(1):
         next(compute)
         next(gather)
     settle = next(gather)

time: 58.6 us -> 58.6 us (level)
  no operation moved by 1% of the time
where the time goes in v6:
time: 58.6 us; the launch traced here: 58.4 us
  Pallas kernels  55.9 us (95%)
  local copies, waits for them, and re-layouts  1.8 us (3%)
  between operations  0.65 us (1%)
    pallas_call x1, Pallas kernels, per_device(): pl.pallas_call(functools.partial(step_kernel, counts), out_shape=(jax.Sha...  54.2 us
    unnamed x4, local copies, waits for them, and re-layouts  1.8 us
    pallas_call x1, Pallas kernels, per_device(): pl.pallas_call(finish_kernel, out_shape=(jax.ShapeDtypeStruct((sx, ry, wi...  1.67 us

profile of v6, /device:TPU:1, one launch (start us, length us, event | category | flops | bytes accessed | tf_op | source)
XLA Modules:
  0.0 58.4 jit_solution(1290964211321630182)
XLA Ops:
  0.6 0.0 copy-start
  0.6 0.9 %copy-done = bf16[1,4,16,8,128]{4,3,2,1,0:T(8,128)(2,1)S(1)} copy-done((bf16[1,4,16,8,128]{4,3,2,1,0:T(8,128)(2,1)S(1)}, bf16[1,4,16,8,128]{4,3,2,1,0:T(8,128)(2,1)}, u32[]{:S(2)}) %copy-start) | copy-done | bytes 131096
  1.5 0.0 copy-start.1
  1.5 0.9 %copy-done.1 = bf16[1,4,16,8,128]{4,3,2,1,0:T(8,128)(2,1)S(1)} copy-done((bf16[1,4,16,8,128]{4,3,2,1,0:T(8,128)(2,1)S(1)}, bf16[1,4,16,8,128]{4,3,2,1,0:T(8,128)(2,1)}, u32[]{:S(2)}) %copy-start.1) | copy-done | bytes 131096
  2.4 54.2 %step.1 = (bf16[4,128,128]{2,1,0:T(8,128)(2,1)S(1)}, bf16[1728,128]{1,0:T(8,128)(2,1)S(1)}, f32[1728,128]{1,0:T(8,128)S(1)}, f32[1728,128]{1,0:T(8,128)S(1)}, f32[1728,128]{1,0:T(8,128)S(1)}) custom-call(bf16[4,128,128]{2,1,0:T(8,128)(2,1)S(1)} %bitcast.3, bf16[4,128,128]{2,1,0:T(8,128)(2,1)S(1)} %bitcast.4, f32[1728,128]{1,0:T(8,128)} %master_hbm.1, ...), custom_call_target="tpu_custom_call" | custom-call | flops 40000000000 | bytes 100000000 | tf_op jit(solution)/shard_map/step/pallas_call | solution.py:638
  56.7 1.7 %finish.1 = (bf16[4,128,128]{2,1,0:T(8,128)(2,1)}, f32[1728,128]{1,0:T(8,128)}, f32[1728,128]{1,0:T(8,128)}, f32[1728,128]{1,0:T(8,128)}) custom-call(bf16[4,128,128]{2,1,0:T(8,128)(2,1)S(1)} %get-tuple-element.13.act_in, bf16[1728,128]{1,0:T(8,128)(2,1)S(1)} %get-tuple-element.14.rows, f32[1728,128]{1,0:T(8,128)S(1)} %get-tuple-element.15.master, ...), custom_call_target="tpu_custom_call" | custom-call | tf_op jit(solution)/shard_map/finish/pallas_call | solution.py:680
Async XLA Ops:
  0.6 0.9 %copy-start = (bf16[1,4,16,8,128]{4,3,2,1,0:T(8,128)(2,1)S(1)}, bf16[1,4,16,8,128]{4,3,2,1,0:T(8,128)(2,1)}, u32[]{:S(2)}) copy-start(bf16[1,4,16,8,128]{4,3,2,1,0:T(8,128)(2,1)} %param.5) | copy-start | bytes 393220
  1.5 0.9 %copy-start.1 = (bf16[1,4,16,8,128]{4,3,2,1,0:T(8,128)(2,1)S(1)}, bf16[1,4,16,8,128]{4,3,2,1,0:T(8,128)(2,1)}, u32[]{:S(2)}) copy-start(bf16[1,4,16,8,128]{4,3,2,1,0:T(8,128)(2,1)} %param.6) | copy-start | bytes 393220
